TPU v7x, 32 devices: a whole 2x2x4 slice. The times are simulated.
32 devices in a mesh: dp: 8 (over y, x, core), tensor: 4 (over z).
Axes of the slice: x: 2, y: 2, z: 4, core: 2. Of those that a mesh axis runs over, the one named last changes fastest.
Arguments:
- x_in: bfloat16 [8192, 1024], P(('dp', 'tensor')), may hold values from -6 to 6
- cotangent: bfloat16 [8192, 1024], P(('dp', 'tensor')), may hold values from -6 to 6
- segments: int32 [8, 1024], P('dp'), may hold values from 0 to 3, as said below
- norm_one: bfloat16 [1024], P('dp'), may hold values from 0.5 to 1.5
- w_query: bfloat16 [1024, 512], P('dp', 'tensor'), may hold values from -0.1875 to 0.1875
- w_keyval: bfloat16 [1024, 256], P('dp'), may hold values from -0.1875 to 0.1875
- w_attn_out: bfloat16 [512, 1024], P('tensor', 'dp'), may hold values from -1 to 1
- w_zgate: bfloat16 [1024, 1536], P('dp', 'tensor'), may hold values from -0.1875 to 0.1875
- w_xin: bfloat16 [1024, 1536], P('dp', 'tensor'), may hold values from -0.1875 to 0.1875
- w_bcin: bfloat16 [1024, 256], P('dp'), may hold values from -0.1875 to 0.1875
- w_dtin: bfloat16 [1024, 24], P('dp', 'tensor'), may hold values from -0.1875 to 0.1875
- conv_x: float32 [4, 1536], P(None, 'tensor'), may hold values from -0.7 to 0.7
- conv_bc: float32 [4, 256], replicated, may hold values from -0.7 to 0.7
- bias_x: float32 [1536], P('tensor'), may hold values from -0.5 to 0.5
- bias_bc: float32 [256], replicated, may hold values from -0.5 to 0.5
- dt_bias: float32 [24], P('tensor'), may hold values from -6.9 to -2.3
- a_log: float32 [24], P('tensor'), may hold values from 0 to 2.77
- d_skip: float32 [24], P('tensor'), may hold values from 0.5 to 1.5
- ssm_gain: float32 [1536], P('tensor'), may hold values from 0.5 to 1.5
- w_mix_out: bfloat16 [1536, 1024], P('tensor', 'dp'), may hold values from -0.15625 to 0.15625
- norm_two: bfloat16 [1024], P('dp'), may hold values from 0.5 to 1.5
- w_gate: bfloat16 [1024, 2048], P('dp', 'tensor'), may hold values from -0.1875 to 0.1875
- w_up: bfloat16 [1024, 2048], P('dp', 'tensor'), may hold values from -0.1875 to 0.1875
- w_down: bfloat16 [2048, 1024], P('tensor', 'dp'), may hold values from -0.125 to 0.125
Outputs:
- block_out: bfloat16 [8192, 1024], P(('dp', 'tensor'))
- grad_input: float32 [8192, 1024], P(('dp', 'tensor'))
- grad_norm_one: float32 [1024], P('dp')
- grad_w_query: float32 [1024, 512], P('dp', 'tensor')
- grad_w_keyval: float32 [1024, 256], P('dp')
- grad_w_attn_out: float32 [512, 1024], P('tensor', 'dp')
- grad_w_zgate: float32 [1024, 1536], P('dp', 'tensor')
- grad_w_xin: float32 [1024, 1536], P('dp', 'tensor')
- grad_w_bcin: float32 [1024, 256], P('dp')
- grad_w_dtin: float32 [1024, 24], P('dp', 'tensor')
- grad_conv_x: float32 [4, 1536], P(None, 'tensor')
- grad_conv_bc: float32 [4, 256], replicated
- grad_bias_x: float32 [1536], P('tensor')
- grad_bias_bc: float32 [256], replicated
- grad_dt_bias: float32 [24], P('tensor')
- grad_a_log: float32 [24], P('tensor')
- grad_d_skip: float32 [24], P('tensor')
- grad_ssm_gain: float32 [1536], P('tensor')
- grad_w_mix_out: float32 [1536, 1024], P('tensor', 'dp')
- grad_norm_two: float32 [1024], P('dp')
- grad_w_gate: float32 [1024, 2048], P('dp', 'tensor')
- grad_w_up: float32 [1024, 2048], P('dp', 'tensor')
- grad_w_down: float32 [2048, 1024], P('tensor', 'dp')
Inputs may be any that keep to these rules, and one draw needn't show every extreme that they name: `segments`: document numbers never fall along a sequence; every sequence holds exactly 4 documents, one of exactly 800 tokens and three of at least 60 tokens each.
All inputs are finite; a program needn't handle non-finite values.
Results may differ from a plain program's by a relative error of at most 0.024.
Values may be sent and summed in bfloat16 or wider, within the bound.
No kernel may reach another device: no remote copies, remote signals or barrier semaphores. Data moves between devices by JAX's collectives and lax.ppermute only.
A program may use at most 128 MiB of HBM per device.

v0:
```python
import math

import jax
import jax.numpy as jnp
from jax import lax
from jax.sharding import PartitionSpec as P

QH = 8
KVH = 2
HD = 64
MH = 24
PD = 64
NS = 128
KW = 4
BLOCK = 128


EPSILON = 1e-05
ROPE_BASE = 100000000000.0
HIGHEST = lax.Precision.HIGHEST


def dense(lhs_mat, rhs_mat):
    return jnp.dot(lhs_mat, rhs_mat, preferred_element_type=jnp.float32)


def dense_nt(lhs_mat, rhs_mat):
    return lax.dot_general(
        lhs_mat, rhs_mat, (((1,), (1,)), ((), ())), preferred_element_type=jnp.float32
    )


def dense_tn(lhs_mat, rhs_mat):
    return lax.dot_general(
        lhs_mat, rhs_mat, (((0,), (0,)), ((), ())), preferred_element_type=jnp.float32
    )


def precise_nt(lhs_mat, rhs_mat):
    return jnp.einsum(
        "rk,dk->rd", lhs_mat, rhs_mat, precision=HIGHEST, preferred_element_type=jnp.float32
    )


def precise_tn(lhs_mat, rhs_mat):
    return jnp.einsum(
        "rd,rk->dk", lhs_mat, rhs_mat, precision=HIGHEST, preferred_element_type=jnp.float32
    )


def rms_scale(values):
    return lax.rsqrt(jnp.mean(values * values, axis=-1, keepdims=True) + EPSILON)


def norm_back(grad_normed, normed, scale):
    return scale * (grad_normed - normed * jnp.mean(grad_normed * normed, axis=-1, keepdims=True))


def gather_rows(values):
    return lax.all_gather(values, "tensor", axis=0, tiled=True)


def sum_rows(values):
    return lax.psum_scatter(
        values.astype(jnp.bfloat16), "tensor", scatter_dimension=0, tiled=True
    ).astype(jnp.float32)


def channel_total(values):
    return lax.psum(jnp.sum(values, axis=-1), "tensor")


def rotate(tensor, length, direction):
    half_dim = HD // 2
    places = jnp.arange(length, dtype=jnp.float32)
    freqs = ROPE_BASE ** (-(jnp.arange(half_dim, dtype=jnp.float32) * (2.0 / HD)))
    angles = places[:, None] * freqs[None, :]
    cosine = jnp.cos(angles)[:, None, :]
    sine_part = direction * jnp.sin(angles)[:, None, :]
    first_half = tensor[..., :half_dim]
    second = tensor[..., half_dim:]
    return jnp.concatenate(
        [first_half * cosine - second * sine_part, second * cosine + first_half * sine_part],
        axis=-1,
    )


def masked_scores(low_query, low_key, segment):
    length = segment.shape[0]
    scores = jnp.einsum(
        "ihd,jhd->hij", low_query, low_key, preferred_element_type=jnp.float32
    ) / math.sqrt(HD)
    positions = jnp.arange(length)
    allowed = (positions[:, None] >= positions[None, :]) & (segment[:, None] == segment[None, :])
    return jnp.where(allowed[None, :, :], scores, -1000000000.0)


def attend_forward(pieces):
    low_query, low_key, low_value, segment = pieces
    masked = masked_scores(low_query, low_key, segment)
    maximum = jnp.max(masked, axis=-1, keepdims=True)
    exponent = jnp.exp(masked - maximum)
    denominator = jnp.sum(exponent, axis=-1, keepdims=True)
    probability = (exponent / denominator).astype(jnp.bfloat16)
    attended = jnp.einsum(
        "hij,jhd->ihd", probability, low_value, preferred_element_type=jnp.float32
    )
    return (attended, maximum[..., 0] + jnp.log(denominator[..., 0]))


def attend_backward(pieces):
    low_query, low_key, low_value, segment, logsum, grad_out = pieces
    masked = masked_scores(low_query, low_key, segment)
    probability = jnp.exp(masked - logsum[:, :, None])
    low_prob = probability.astype(jnp.bfloat16)
    grad_prob = jnp.einsum("ihd,jhd->hij", grad_out, low_value, preferred_element_type=jnp.float32)
    grad_scores = probability * (
        grad_prob - jnp.sum(grad_prob * probability, axis=-1, keepdims=True)
    )
    low_grad = grad_scores.astype(jnp.bfloat16)
    grad_query = jnp.einsum(
        "hij,jhd->ihd", low_grad, low_key, preferred_element_type=jnp.float32
    ) / math.sqrt(HD)
    grad_key = jnp.einsum(
        "hij,ihd->jhd", low_grad, low_query, preferred_element_type=jnp.float32
    ) / math.sqrt(HD)
    grad_value = jnp.einsum("hij,ihd->jhd", low_prob, grad_out, preferred_element_type=jnp.float32)
    return (grad_query, grad_key, grad_value)


def conv_silu(values, weight, bias_vec, segment):
    length = values.shape[1]
    accumulated = bias_vec[None, None, :] + weight[KW - 1][None, None, :] * values
    for offset in range(1, KW):
        shifted = jnp.pad(values, ((0, 0), (offset, 0), (0, 0)))[:, :length]
        linked = jnp.pad(segment, ((0, 0), (offset, 0)), constant_values=-1)[:, :length] == segment
        accumulated = accumulated + weight[KW - 1 - offset][None, None, :] * shifted * linked[
            :, :, None
        ].astype(jnp.float32)
    return jax.nn.silu(accumulated)


def ssd_core(x_conv, bc_conv, dt_raw, gate_z, segment, dt_bias, a_log, d_skip):
    length, channels = x_conv.shape
    head_num = dt_raw.shape[1]
    block_num = length // BLOCK
    steps_all = jax.nn.softplus(dt_raw + dt_bias[None, :])
    logdecay = -steps_all * jnp.exp(a_log)[None, :]
    pieces = (
        x_conv.reshape(block_num, BLOCK, head_num, PD),
        bc_conv[:, :NS].reshape(block_num, BLOCK, NS),
        bc_conv[:, NS:].reshape(block_num, BLOCK, NS),
        steps_all.reshape(block_num, BLOCK, head_num),
        logdecay.reshape(block_num, BLOCK, head_num),
        segment.reshape(block_num, BLOCK),
    )

    def one_block(carry, blocks):
        carried_state, last_segment = carry
        x_blk, b_blk, c_blk, step_blk, logdecay_blk, seg_blk = blocks
        cumlog = jnp.cumsum(logdecay_blk, axis=0)
        positions = jnp.arange(BLOCK)
        linked = (positions[:, None] >= positions[None, :]) & (seg_blk[:, None] == seg_blk[None, :])
        gaps = jnp.where(linked[:, :, None], cumlog[:, None, :] - cumlog[None, :, :], 0.0)
        decays = jnp.exp(gaps) * linked[:, :, None].astype(jnp.float32)
        contact = jnp.dot(c_blk, b_blk.T, precision=HIGHEST, preferred_element_type=jnp.float32)
        mixing = decays * contact[:, :, None] * step_blk[None, :, :]
        within = jnp.einsum("ijh,jhp->ihp", mixing, x_blk, precision=HIGHEST)
        entering = jnp.exp(cumlog) * (seg_blk == last_segment).astype(jnp.float32)[:, None]
        from_state = (
            jnp.einsum("in,hpn->ihp", c_blk, carried_state, precision=HIGHEST)
            * entering[:, :, None]
        )
        outputs = within + from_state + d_skip[None, :, None] * x_blk
        tailing = (seg_blk == seg_blk[BLOCK - 1]).astype(jnp.float32)
        weights_tail = jnp.exp(cumlog[BLOCK - 1][None, :] - cumlog) * tailing[:, None] * step_blk
        kept_share = jnp.exp(cumlog[BLOCK - 1]) * (seg_blk[BLOCK - 1] == last_segment).astype(
            jnp.float32
        )
        next_state = (
            jnp.einsum("jh,jhp,jn->hpn", weights_tail, x_blk, b_blk, precision=HIGHEST)
            + carried_state * kept_share[:, None, None]
        )
        return ((next_state, seg_blk[BLOCK - 1]), outputs)

    initial = (jnp.zeros((head_num, PD, NS), jnp.float32), jnp.int32(-1))
    unused, outputs = lax.scan(jax.checkpoint(one_block), initial, pieces)
    return outputs.reshape(length, channels) * jax.nn.silu(gate_z)


def local(
    x_in,
    cotangent,
    segments,
    norm_one,
    w_query,
    w_keyval,
    w_attn_out,
    w_zgate,
    w_xin,
    w_bcin,
    w_dtin,
    conv_x,
    conv_bc,
    bias_x,
    bias_bc,
    dt_bias,
    a_log,
    d_skip,
    ssm_gain,
    w_mix_out,
    norm_two,
    w_gate,
    w_up,
    w_down,
):
    (
        gain_one,
        gain_two,
        query_w,
        keyval_w,
        zgate_w,
        xin_w,
        bcin_w,
        dtin_w,
        gate_w,
        upper_w,
        attn_w,
        mix_w,
        down_w,
    ) = (
        lax.all_gather(norm_one, "dp", axis=0, tiled=True),
        lax.all_gather(norm_two, "dp", axis=0, tiled=True),
        lax.all_gather(w_query, "dp", axis=0, tiled=True),
        lax.all_gather(w_keyval, "dp", axis=0, tiled=True),
        lax.all_gather(w_zgate, "dp", axis=0, tiled=True),
        lax.all_gather(w_xin, "dp", axis=0, tiled=True),
        lax.all_gather(w_bcin, "dp", axis=0, tiled=True),
        lax.all_gather(w_dtin, "dp", axis=0, tiled=True),
        lax.all_gather(w_gate, "dp", axis=0, tiled=True),
        lax.all_gather(w_up, "dp", axis=0, tiled=True),
        lax.all_gather(w_attn_out, "dp", axis=1, tiled=True),
        lax.all_gather(w_mix_out, "dp", axis=1, tiled=True),
        lax.all_gather(w_down, "dp", axis=1, tiled=True),
    )
    seq_count = segments.shape[0]
    length = segments.shape[1]
    width_ssm = MH * PD
    gain_one_f = gain_one.astype(jnp.float32)
    gain_two_f = gain_two.astype(jnp.float32)
    residual = x_in.astype(jnp.float32)
    scale_one = rms_scale(residual)
    normed_one = residual * scale_one
    rows_one = gather_rows((normed_one * gain_one_f[None, :]).astype(jnp.bfloat16))
    queries = dense(rows_one, query_w)
    keyvals = dense(rows_one, keyval_w)
    zgate = dense(rows_one, zgate_w)
    xin_raw = dense(rows_one, xin_w)
    bc_raw = dense(rows_one, bcin_w)
    dt_raw = dense(rows_one, dtin_w)
    head_count = query_w.shape[1] // HD
    head_ids = lax.axis_index("tensor") * head_count + jnp.arange(head_count)
    head_map = ((head_ids // (QH // KVH))[:, None] == jnp.arange(KVH)[None, :]).astype(jnp.float32)
    key_all = keyvals[:, : KVH * HD].reshape(seq_count, length, KVH, HD)
    value_all = keyvals[:, KVH * HD :].reshape(seq_count, length, KVH, HD)
    low_query = rotate(queries.reshape(seq_count, length, head_count, HD), length, 1.0).astype(
        jnp.bfloat16
    )
    low_key = rotate(
        jnp.einsum("slkd,hk->slhd", key_all, head_map, precision=HIGHEST), length, 1.0
    ).astype(jnp.bfloat16)
    low_value = jnp.einsum("slkd,hk->slhd", value_all, head_map, precision=HIGHEST).astype(
        jnp.bfloat16
    )
    attended, logsum = lax.map(attend_forward, (low_query, low_key, low_value, segments))
    attn_low = attended.reshape(-1, head_count * HD).astype(jnp.bfloat16)

    def conv_of_x(values, weight, bias_vec):
        return conv_silu(values, weight, bias_vec, segments)

    x_conv, conv_x_back = jax.vjp(conv_of_x, xin_raw.reshape(seq_count, length, -1), conv_x, bias_x)
    bc_conv, conv_bc_back = jax.vjp(
        conv_of_x, bc_raw.reshape(seq_count, length, -1), conv_bc, bias_bc
    )

    def scan_all(x_vals, bc_vals, dt_vals, gate_vals, bias_dt, log_rate, skip_vals):

        def scan_one(pieces):
            return ssd_core(
                pieces[0], pieces[1], pieces[2], pieces[3], pieces[4], bias_dt, log_rate, skip_vals
            )

        return lax.map(jax.checkpoint(scan_one), (x_vals, bc_vals, dt_vals, gate_vals, segments))

    gated, scan_back = jax.vjp(
        scan_all,
        x_conv.astype(jnp.bfloat16).astype(jnp.float32),
        bc_conv.astype(jnp.bfloat16).astype(jnp.float32),
        dt_raw.reshape(seq_count, length, -1),
        zgate.reshape(seq_count, length, -1),
        dt_bias,
        a_log,
        d_skip,
    )
    gated = gated.reshape(-1, gated.shape[-1])
    scale_ssm = lax.rsqrt(channel_total(gated * gated) / width_ssm + EPSILON)[:, None]
    normed_ssm = gated * scale_ssm
    mixed_low = (normed_ssm * ssm_gain[None, :]).astype(jnp.bfloat16)
    middle = residual + sum_rows(dense(attn_low, attn_w) + dense(mixed_low, mix_w))
    scale_two = rms_scale(middle)
    normed_two = middle * scale_two
    rows_two = gather_rows((normed_two * gain_two_f[None, :]).astype(jnp.bfloat16))
    gate_pre = dense(rows_two, gate_w)
    up_pre = dense(rows_two, upper_w)
    silu_gate = jax.nn.silu(gate_pre)
    hidden = (silu_gate * up_pre).astype(jnp.bfloat16)
    block_out = (middle + sum_rows(dense(hidden, down_w))).astype(jnp.bfloat16)
    grad_rows = gather_rows(cotangent)
    grad_hidden = dense_nt(grad_rows, down_w)
    grad_down = dense_tn(hidden, grad_rows)
    sigmoid_gate = jax.nn.sigmoid(gate_pre)
    grad_gate = (
        grad_hidden * up_pre * sigmoid_gate * (1.0 + gate_pre * (1.0 - sigmoid_gate))
    ).astype(jnp.bfloat16)
    grad_upper = (grad_hidden * silu_gate).astype(jnp.bfloat16)
    grad_gate_w = dense_tn(rows_two, grad_gate)
    grad_upper_w = dense_tn(rows_two, grad_upper)
    grad_two = sum_rows(dense_nt(grad_gate, gate_w) + dense_nt(grad_upper, upper_w))
    grad_gain_two = jnp.sum(grad_two * normed_two, axis=0)
    grad_middle = cotangent.astype(jnp.float32) + norm_back(
        grad_two * gain_two_f[None, :], normed_two, scale_two
    )
    grad_branch = gather_rows(grad_middle.astype(jnp.bfloat16))
    grad_attn = (
        dense_nt(grad_branch, attn_w)
        .astype(jnp.bfloat16)
        .reshape(seq_count, length, head_count, HD)
    )
    grad_attn_w = dense_tn(attn_low, grad_branch)
    grad_mixed = dense_nt(grad_branch, mix_w)
    grad_mix_w = dense_tn(mixed_low, grad_branch)
    grad_gain_ssm = jnp.sum(grad_mixed * normed_ssm, axis=0)
    grad_normed_ssm = grad_mixed * ssm_gain[None, :]
    row_inner = channel_total(grad_normed_ssm * normed_ssm)
    grad_gated = scale_ssm * (grad_normed_ssm - normed_ssm * (row_inner / width_ssm)[:, None])
    grad_xconv, grad_bcconv, grad_dt, grad_zgate, grad_dt_bias, grad_a_log, grad_d_skip = scan_back(
        grad_gated.reshape(seq_count, length, -1)
    )
    grad_xin, grad_conv_x, grad_bias_x = conv_x_back(grad_xconv)
    grad_bc, grad_conv_bc, grad_bias_bc = conv_bc_back(grad_bcconv)
    grad_lq, grad_lk, grad_lv = lax.map(
        attend_backward, (low_query, low_key, low_value, segments, logsum, grad_attn)
    )
    grad_query = rotate(grad_lq, length, -1.0).reshape(-1, head_count * HD).astype(jnp.bfloat16)
    grad_key = jnp.einsum(
        "slhd,hk->slkd", rotate(grad_lk, length, -1.0), head_map, precision=HIGHEST
    )
    grad_val = jnp.einsum("slhd,hk->slkd", grad_lv, head_map, precision=HIGHEST)
    grad_keyval = jnp.concatenate(
        [grad_key.reshape(-1, KVH * HD), grad_val.reshape(-1, KVH * HD)], axis=1
    )
    low_zgate = grad_zgate.reshape(-1, grad_zgate.shape[-1]).astype(jnp.bfloat16)
    low_xin = grad_xin.reshape(-1, grad_xin.shape[-1]).astype(jnp.bfloat16)
    low_dt = grad_dt.reshape(-1, grad_dt.shape[-1]).astype(jnp.bfloat16)
    grad_bc_rows = grad_bc.reshape(-1, 2 * NS)
    grad_one = sum_rows(
        dense_nt(grad_query, query_w)
        + dense_nt(low_zgate, zgate_w)
        + dense_nt(low_xin, xin_w)
        + dense_nt(low_dt, dtin_w)
        + precise_nt(grad_keyval, keyval_w)
        + precise_nt(grad_bc_rows, bcin_w)
    )
    grad_gain_one = jnp.sum(grad_one * normed_one, axis=0)
    grad_input = grad_middle + norm_back(grad_one * gain_one_f[None, :], normed_one, scale_one)
    grad_query_w = dense_tn(rows_one, grad_query)
    grad_keyval_w = precise_tn(rows_one, grad_keyval)
    grad_zgate_w = dense_tn(rows_one, low_zgate)
    grad_xin_w = dense_tn(rows_one, low_xin)
    grad_bcin_w = precise_tn(rows_one, grad_bc_rows)
    grad_dtin_w = dense_tn(rows_one, low_dt)
    every_part = (
        lax.psum_scatter(grad_gain_one, "dp", scatter_dimension=0, tiled=True),
        lax.psum_scatter(grad_query_w, "dp", scatter_dimension=0, tiled=True),
        lax.psum_scatter(grad_keyval_w, "dp", scatter_dimension=0, tiled=True),
        lax.psum_scatter(grad_zgate_w, "dp", scatter_dimension=0, tiled=True),
        lax.psum_scatter(grad_xin_w, "dp", scatter_dimension=0, tiled=True),
        lax.psum_scatter(grad_bcin_w, "dp", scatter_dimension=0, tiled=True),
        lax.psum_scatter(grad_dtin_w, "dp", scatter_dimension=0, tiled=True),
        lax.psum_scatter(grad_attn_w, "dp", scatter_dimension=1, tiled=True),
        lax.psum_scatter(grad_mix_w, "dp", scatter_dimension=1, tiled=True),
        lax.psum_scatter(grad_gain_two, "dp", scatter_dimension=0, tiled=True),
        lax.psum_scatter(grad_gate_w, "dp", scatter_dimension=0, tiled=True),
        lax.psum_scatter(grad_upper_w, "dp", scatter_dimension=0, tiled=True),
        lax.psum_scatter(grad_down, "dp", scatter_dimension=1, tiled=True),
    )
    mixer_parts = every_part[:9]
    ffn_parts = every_part[9:]
    small = lax.psum(
        (
            grad_conv_x,
            grad_bias_x,
            grad_dt_bias,
            grad_a_log,
            grad_d_skip,
            grad_gain_ssm,
            grad_conv_bc,
            grad_bias_bc,
        ),
        "dp",
    )
    shared = (
        lax.psum(mixer_parts[0].astype(jnp.bfloat16), "tensor").astype(jnp.float32),
        lax.psum(ffn_parts[0].astype(jnp.bfloat16), "tensor").astype(jnp.float32),
        lax.psum(mixer_parts[2].astype(jnp.bfloat16), "tensor").astype(jnp.float32),
        lax.psum(mixer_parts[5].astype(jnp.bfloat16), "tensor").astype(jnp.float32),
        lax.psum(small[6].astype(jnp.bfloat16), "tensor").astype(jnp.float32),
        lax.psum(small[7].astype(jnp.bfloat16), "tensor").astype(jnp.float32),
    )
    return (
        block_out,
        grad_input,
        shared[0],
        mixer_parts[1],
        shared[2],
        mixer_parts[7],
        mixer_parts[3],
        mixer_parts[4],
        shared[3],
        mixer_parts[6],
        small[0],
        shared[4],
        small[1],
        shared[5],
        small[2],
        small[3],
        small[4],
        small[5],
        mixer_parts[8],
        shared[1],
        ffn_parts[1],
        ffn_parts[2],
        ffn_parts[3],
    )


def solution(mesh):
    return jax.shard_map(
        local,
        mesh=mesh,
        in_specs=(
            P(("dp", "tensor"), None),
            P(("dp", "tensor"), None),
            P("dp", None),
            P("dp"),
            P("dp", "tensor"),
            P("dp", None),
            P("tensor", "dp"),
            P("dp", "tensor"),
            P("dp", "tensor"),
            P("dp", None),
            P("dp", "tensor"),
            P(None, "tensor"),
            P(),
            P("tensor"),
            P(),
            P("tensor"),
            P("tensor"),
            P("tensor"),
            P("tensor"),
            P("tensor", "dp"),
            P("dp"),
            P("dp", "tensor"),
            P("dp", "tensor"),
            P("tensor", "dp"),
        ),
        out_specs=(
            P(("dp", "tensor"), None),
            P(("dp", "tensor"), None),
            P("dp"),
            P("dp", "tensor"),
            P("dp", None),
            P("tensor", "dp"),
            P("dp", "tensor"),
            P("dp", "tensor"),
            P("dp", None),
            P("dp", "tensor"),
            P(None, "tensor"),
            P(),
            P("tensor"),
            P(),
            P("tensor"),
            P("tensor"),
            P("tensor"),
            P("tensor"),
            P("tensor", "dp"),
            P("dp"),
            P("dp", "tensor"),
            P("dp", "tensor"),
            P("tensor", "dp"),
        ),
        check_vma=False,
    )
```

profile of v0, /device:TPU:0, one launch (start us, length us, event | category | flops | bytes accessed | tf_op | source)
XLA Modules:
  0.0 1839.3 jit_solution(9117631873077088337)
XLA Ops:
  8.1 10.3 all-gather
  22.4 8.8 all_gather.58
  31.2 9.4 all_gather.54
  40.6 9.4 all_gather.55
  50.1 9.0 all_gather.53
  59.1 9.8 all_gather.57
  69.0 10.9 all_gather.56
  79.9 10.9 all_gather.59
  90.7 11.1 all_gather.60
  133.5 139.6 %while.103 = (s32[]{:T(128)}, f32[6,64,128]{2,1,0:T(8,128)S(1)}, s32[]{:T(128)}, f32[8,128,6,64]{1,0,3,2:T(8,128)}, f32[8,128,6,64]{1,0,3,2:T(8,128)}, /*index=5...) while((s32[]{:T(128)}, f32[6,64,128]{2,1,0:T(8,128)S(1)}, ...), condition=%wide.region_5.6_spmd.clone, body=%wide.region_3.5_spmd.clone.sunk | while | flops 252709632 | bytes 3854741 | solution.py:187
  143.1 6.1 dynamic_update_slice.115
  160.6 6.1 dynamic_update_slice.115
  178.0 6.1 dynamic_update_slice.115
  195.5 6.1 dynamic_update_slice.115
  212.9 6.1 dynamic_update_slice.115
  230.4 6.1 dynamic_update_slice.115
  247.8 6.1 dynamic_update_slice.115
  265.3 6.1 dynamic_update_slice.115
  277.8 12.2 psum.112
  304.2 8.3 all-gather.1
  312.5 32.3 %reduce-scatter.16.cloned.1.call-done = bf16[256,1024]{1,0:T(8,128)(2,1)} async-done(((bf16[1024,1024]{1,0:T(8,128)(2,1)}), bf16[256,1024]{1,0:T(8,128)(2,1)}) %reduce-scatter.16.cloned.1.call-update) | async-done | bytes 524304 | tf_op jit(solution)/shard_map/reduce_scatter | solution.py:64
  350.5 42.6 %all-gather.12.cloned.1.call-done = bf16[1024,1024]{1,0:T(8,128)(2,1)} async-done(((bf16[256,1024]{1,0:T(8,128)(2,1)}), bf16[1024,1024]{1,0:T(8,128)(2,1)}) %all-gather.12.cloned.1.call-update) | async-done | bytes 2097168 | tf_op jit(solution)/shard_map/all_gather | solution.py:60
  397.6 19.7 %all-gather.16.cloned.1.call-done = bf16[1024,512]{1,0:T(8,128)(2,1)} async-done(((bf16[128,512]{1,0:T(8,128)(2,1)}), bf16[1024,512]{1,0:T(8,128)(2,1)}) %all-gather.16.cloned.1.call-update) | async-done | bytes 1048592 | tf_op jit(solution)/shard_map/all_gather | solution.py:241
  421.8 20.9 %all-gather.18.cloned.1.call-done = bf16[512,1024]{1,0:T(8,128)(2,1)} async-done(((bf16[512,128]{1,0:T(8,128)(2,1)}), bf16[512,1024]{1,0:T(8,128)(2,1)}) %all-gather.18.cloned.1.call-update) | async-done | bytes 1048592 | tf_op jit(solution)/shard_map/all_gather | solution.py:244
  442.7 47.3 %all-gather.20.cloned.1.call-done = bf16[1024,1024]{1,0:T(8,128)(2,1)} async-done(((bf16[256,1024]{1,0:T(8,128)(2,1)}), bf16[1024,1024]{1,0:T(8,128)(2,1)}) %all-gather.20.cloned.1.call-update) | async-done | bytes 2097168 | tf_op jit(solution)/shard_map/all_gather | solution.py:60
  490.0 6.4 multiply_convert_fusion.1
  501.0 42.8 %reduce-scatter.20.cloned.1.call-done = bf16[256,1024]{1,0:T(8,128)(2,1)} async-done(((bf16[1024,1024]{1,0:T(8,128)(2,1)}), bf16[256,1024]{1,0:T(8,128)(2,1)}) %reduce-scatter.20.cloned.1.call-update) | async-done | bytes 524304 | tf_op jit(solution)/shard_map/reduce_scatter | solution.py:64
  547.7 45.0 %all-gather.22.cloned.1.call-done = bf16[1024,1024]{1,0:T(8,128)(2,1)} async-done(((bf16[256,1024]{1,0:T(8,128)(2,1)}), bf16[1024,1024]{1,0:T(8,128)(2,1)}) %all-gather.22.cloned.1.call-update) | async-done | bytes 2097168 | tf_op jit(solution)/shard_map/all_gather | solution.py:60
  595.2 5.1 multiply_reduce_fusion.5
  612.6 9.5 psum.113
  636.2 154.9 %while.104 = (s32[]{:T(128)}, f32[6,64,128]{2,1,0:T(8,128)S(1)}, s32[]{:T(128)}, f32[8,128,6,64]{1,0,3,2:T(8,128)}, f32[8,6,64,128]{3,2,1,0:T(8,128)}, /*index=5...) while((s32[]{:T(128)}, f32[6,64,128]{2,1,0:T(8,128)S(1)}, ...), condition=%wide.region_18.19_spmd.clone, body=%wide.region_16.18_spmd.clone.sunk | while | flops 252807936 | bytes 3192699 | solution.py:187
  645.2 6.1 dynamic_update_slice.117
  664.5 6.1 dynamic_update_slice.117
  683.8 6.1 dynamic_update_slice.117
  703.1 6.1 dynamic_update_slice.117
  722.4 6.1 dynamic_update_slice.117
  741.7 6.1 dynamic_update_slice.117
  761.0 6.1 dynamic_update_slice.117
  780.3 6.1 dynamic_update_slice.117
  801.4 445.0 %while.105 = (s32[]{:T(128)}, f32[6]{0:T(128)}, f32[6,64,128]{2,1,0:T(8,128)}, f32[8,128,6,64]{1,0,3,2:T(8,128)}, f32[8,128,128]{2,1,0:T(8,128)}, /*index=5*/f32...) while((s32[]{:T(128)}, f32[6]{0:T(128)}, ...), condition=%wide.region_30.31_spmd.clone, body=%wide.region_19.30_spmd.clone.sunk | while | flops 607123456 | bytes 8248718 | solution.py:187
  848.6 6.1 dynamic_update_slice.122
  904.4 6.1 dynamic_update_slice.122
  960.1 6.1 dynamic_update_slice.122
  1015.9 6.1 dynamic_update_slice.122
  1071.6 6.1 dynamic_update_slice.122
  1127.3 6.1 dynamic_update_slice.122
  1183.1 6.1 dynamic_update_slice.122
  1238.8 6.1 dynamic_update_slice.122
  1288.9 5.6 fusion.154
  1305.5 24.7 %reduce-scatter.26.cloned.1.call-done = f32[128,256]{1,0:T(8,128)} async-done(((f32[1024,256]{1,0:T(8,128)}), f32[128,256]{1,0:T(8,128)}) %reduce-scatter.26.cloned.1.call-update) | async-done | bytes 131088 | tf_op jit(solution)/shard_map/reduce_scatter | solution.py:385
  1332.1 11.6 add_convert_fusion
  1385.2 27.1 %reduce-scatter.22.cloned.1.call-done = bf16[256,1024]{1,0:T(8,128)(2,1)} async-done(((bf16[1024,1024]{1,0:T(8,128)(2,1)}), bf16[256,1024]{1,0:T(8,128)(2,1)}) %reduce-scatter.22.cloned.1.call-update) | async-done | bytes 524304 | tf_op jit(solution)/shard_map/reduce_scatter | solution.py:64
  1413.9 24.5 %all-reduce.29 = (bf16[1024]{0:T(1024)(128)(2,1)S(1)}, f32[4,384]{1,0:T(4,128)}, bf16[4,256]{1,0:T(4,128)(2,1)S(1)}, f32[384]{0:T(512)}, bf16[256]{0:T(256)(128)...) all-reduce(f32[1024]{0:T(1024)S(1)} %get-tuple-element.1079, ...), channel_id=6, replica_groups=mesh['dp'=8,'tensor'=4] {'dp'}, use_global_device_ids=true, to_apply=%region_34.35.clone | all-reduce | flops 5650 | bytes 38544
  1438.6 11.2 all-reduce.30
  1452.0 6.1 reduce-scatter.18.cloned.1.call-done
  1461.3 41.6 %reduce-scatter.40.cloned.1.call-done = f32[128,512]{1,0:T(8,128)} async-done(((f32[1024,512]{1,0:T(8,128)}), f32[128,512]{1,0:T(8,128)}) %reduce-scatter.40.cloned.1.call-update) | async-done | bytes 262160 | tf_op jit(solution)/shard_map/reduce_scatter | solution.py:393
  1502.9 45.1 %reduce-scatter.42.cloned.1.call-done = f32[128,512]{1,0:T(8,128)} async-done(((f32[1024,512]{1,0:T(8,128)}), f32[128,512]{1,0:T(8,128)}) %reduce-scatter.42.cloned.1.call-update) | async-done | bytes 262160 | tf_op jit(solution)/shard_map/reduce_scatter | solution.py:394
  1548.1 45.3 %reduce-scatter.44.cloned.1.call-done = f32[512,128]{1,0:T(8,128)} async-done(((f32[512,1024]{1,0:T(8,128)}), f32[512,128]{1,0:T(8,128)}) %reduce-scatter.44.cloned.1.call-update) | async-done | bytes 262160 | tf_op jit(solution)/shard_map/reduce_scatter | solution.py:395
  1593.4 34.9 %reduce-scatter.36.cloned.1.call-done = f32[128,6]{0,1:T(8,128)} async-done(((f32[1024,6]{0,1:T(8,128)}), f32[128,6]{0,1:T(8,128)}) %reduce-scatter.36.cloned.1.call-update) | async-done | bytes 3088 | tf_op jit(solution)/shard_map/reduce_scatter | solution.py:389
  1628.3 38.0 %reduce-scatter.24.cloned.1.call-done = f32[128,128]{1,0:T(8,128)} async-done(((f32[1024,128]{1,0:T(8,128)}), f32[128,128]{1,0:T(8,128)}) %reduce-scatter.24.cloned.1.call-update) | async-done | bytes 65552 | tf_op jit(solution)/shard_map/reduce_scatter | solution.py:384
  1666.3 37.8 %reduce-scatter.28.cloned.1.call-done = f32[128,128]{1,0:T(8,128)} async-done(((f32[128,1024]{1,0:T(8,128)}), f32[128,128]{1,0:T(8,128)}) %reduce-scatter.28.cloned.1.call-update) | async-done | bytes 65552 | tf_op jit(solution)/shard_map/reduce_scatter | solution.py:390
  1704.1 42.6 %reduce-scatter.38.cloned.1.call-done = f32[384,128]{1,0:T(8,128)} async-done(((f32[384,1024]{1,0:T(8,128)}), f32[384,128]{1,0:T(8,128)}) %reduce-scatter.38.cloned.1.call-update) | async-done | bytes 196624 | tf_op jit(solution)/shard_map/reduce_scatter | solution.py:391
  1746.6 42.5 %reduce-scatter.32.cloned.1.call-done = f32[128,384]{1,0:T(8,128)} async-done(((f32[1024,384]{1,0:T(8,128)}), f32[128,384]{1,0:T(8,128)}) %reduce-scatter.32.cloned.1.call-update) | async-done | bytes 196624 | tf_op jit(solution)/shard_map/reduce_scatter | solution.py:387
  1789.1 42.5 %reduce-scatter.30.cloned.1.call-done = f32[128,384]{1,0:T(8,128)} async-done(((f32[1024,384]{1,0:T(8,128)}), f32[128,384]{1,0:T(8,128)}) %reduce-scatter.30.cloned.1.call-update) | async-done | bytes 196624 | tf_op jit(solution)/shard_map/reduce_scatter | solution.py:386
  (1311 shorter events, 778.1 us)
Async XLA Ops:
  8.0 23.2 %copy-start.90 = (bf16[128,128]{1,0:T(8,128)(2,1)S(1)}, bf16[128,128]{1,0:T(8,128)(2,1)}, u32[]{:S(2)}) copy-start(bf16[128,128]{1,0:T(8,128)(2,1)} %param.34) | copy-start | bytes 98308
  8.1 32.5 %copy-start.91 = (bf16[128,128]{1,0:T(8,128)(2,1)S(1)}, bf16[128,128]{1,0:T(8,128)(2,1)}, u32[]{:S(2)}) copy-start(bf16[128,128]{1,0:T(8,128)(2,1)} %param.36) | copy-start | bytes 98308
  8.1 42.0 %copy-start.124 = (f32[4,384]{1,0:T(4,128)S(1)}, f32[4,384]{1,0:T(4,128)}, u32[]{:S(2)}) copy-start(f32[4,384]{1,0:T(4,128)} %param.41) | copy-start | bytes 18436
  8.1 42.0 %copy-start.83 = (bf16[128,256]{1,0:T(8,128)(2,1)S(1)}, bf16[128,256]{1,0:T(8,128)(2,1)}, u32[]{:S(2)}) copy-start(bf16[128,256]{1,0:T(8,128)(2,1)} %param.35) | copy-start | bytes 196612
  8.1 98.3 %all-gather.10.cloned.1.call-start = ((), (), s32[]{:S(2)}) async-start(), calls=%async_computation.15 | async-start | bytes 2621440 | tf_op jit(solution)/shard_map/all_gather | solution.py:60
  18.5 31.6 %copy-start.85 = (f32[8,1,128]{2,1,0:T(1,128)}, f32[8,1,128]{2,1,0:T(1,128)S(1)}, u32[]{:S(2)}) copy-start(f32[8,1,128]{2,1,0:T(1,128)S(1)} %convert_element_type.362) | copy-start | bytes 12292
  18.5 40.7 %copy-start.84 = (bf16[128,256]{1,0:T(8,128)(2,1)S(1)}, bf16[128,256]{1,0:T(8,128)(2,1)}, u32[]{:S(2)}) copy-start(bf16[128,256]{1,0:T(8,128)(2,1)} %param.39) | copy-start | bytes 196612
  19.7 49.2 %copy-start.80 = (bf16[128,384]{1,0:T(8,128)(2,1)S(1)}, bf16[128,384]{1,0:T(8,128)(2,1)}, u32[]{:S(2)}) copy-start(bf16[128,384]{1,0:T(8,128)(2,1)} %param.38) | copy-start | bytes 294916
  21.8 58.0 %copy-start.81 = (bf16[128,384]{1,0:T(8,128)(2,1)S(1)}, bf16[128,384]{1,0:T(8,128)(2,1)}, u32[]{:S(2)}) copy-start(bf16[128,384]{1,0:T(8,128)(2,1)} %param.37) | copy-start | bytes 294916
  21.8 322.9 %reduce-scatter.16.cloned.1.call-start = ((), (), s32[]{:S(2)}) async-start(), calls=%async_computation.16 | async-start | bytes 2621440 | tf_op jit(solution)/shard_map/reduce_scatter | solution.py:64
  31.2 99.6 %copy-start.71 = (bf16[1024,6]{0,1:T(8,128)(2,1)}, bf16[1024,6]{0,1:T(8,128)(2,1)S(1)}, u32[]{:S(2)}) copy-start(bf16[1024,6]{0,1:T(8,128)(2,1)S(1)} %all_gather.58) | copy-start | bytes 36868
  40.6 50.1 %copy-start.82 = (bf16[384,128]{1,0:T(8,128)(2,1)S(1)}, bf16[384,128]{1,0:T(8,128)(2,1)}, u32[]{:S(2)}) copy-start(bf16[384,128]{1,0:T(8,128)(2,1)} %param.49) | copy-start | bytes 294916
  50.0 61.3 %copy-start.125 = (s32[2]{0:T(128)}, s32[2]{0:T(128)S(1)}, u32[]{:S(2)}) copy-start(s32[2]{0:T(128)S(1)} %and_select_fusion) | copy-start | bytes 28
  50.1 69.6 %copy-start.94 = (f32[384]{0:T(512)}, f32[384]{0:T(512)S(1)}, u32[]{:S(2)}) copy-start(f32[384]{0:T(512)S(1)} %get-tuple-element.1084) | copy-start | bytes 4612
  50.1 69.6 %copy-start.96 = (f32[384]{0:T(512)}, f32[384]{0:T(512)S(1)}, u32[]{:S(2)}) copy-start(f32[384]{0:T(512)S(1)} %get-tuple-element.1085) | copy-start | bytes 4612
  50.1 69.6 %copy-start.98 = (f32[384]{0:T(512)}, f32[384]{0:T(512)S(1)}, u32[]{:S(2)}) copy-start(f32[384]{0:T(512)S(1)} %get-tuple-element.1086) | copy-start | bytes 4612
  50.1 69.6 %copy-start.103 = (f32[384]{0:T(512)}, f32[384]{0:T(512)S(1)}, u32[]{:S(2)}) copy-start(f32[384]{0:T(512)S(1)} %get-tuple-element.1083) | copy-start | bytes 4612
  59.1 47.3 %copy-start.19 = (bf16[1024,256]{1,0:T(8,128)(2,1)}, bf16[1024,256]{1,0:T(8,128)(2,1)S(1)}, u32[]{:S(2)}) copy-start(bf16[1024,256]{1,0:T(8,128)(2,1)S(1)} %all_gather.53) | copy-start | bytes 1572868
  59.1 42.7 %copy-start.130 = (f32[4,256]{1,0:T(4,128)S(1)}, f32[4,256]{1,0:T(4,128)}, u32[]{:S(2)}) copy-start(f32[4,256]{1,0:T(4,128)} %param.42) | copy-start | bytes 12292
  69.0 44.6 %copy-start.35 = (bf16[1024,256]{1,0:T(8,128)(2,1)}, bf16[1024,256]{1,0:T(8,128)(2,1)S(1)}, u32[]{:S(2)}) copy-start(bf16[1024,256]{1,0:T(8,128)(2,1)S(1)} %all_gather.57) | copy-start | bytes 1572868
  102.8 17.0 copy-start.63
  102.8 17.0 copy-start.65
  104.1 186.8 %copy-start.39 = (f32[1024,32]{0,1:T(8,128)}, f32[1024,32]{0,1:T(8,128)S(1)}, u32[]{:S(2)}) copy-start(f32[1024,32]{0,1:T(8,128)S(1)} %get-tuple-element.1271) | copy-start | bytes 393220
  273.0 17.0 copy-start.33
  290.0 332.1 %copy-start.88 = (f32[1024]{0:T(1024)}, f32[1024]{0:T(1024)S(1)}, u32[]{:S(2)}) copy-start(f32[1024]{0:T(1024)S(1)} %add_rsqrt_fusion) | copy-start | bytes 12292
  303.5 41.3 %copy-start.2 = (bf16[256,1024]{1,0:T(8,128)(2,1)S(1)}, bf16[256,1024]{1,0:T(8,128)(2,1)}, u32[]{:S(2)}) copy-start(bf16[256,1024]{1,0:T(8,128)(2,1)} %param.30) | copy-start | bytes 1572868
  303.6 47.0 %all-gather.14.cloned.1.call-start = ((), (), s32[]{:S(2)}) async-start(), calls=%async_computation.18 | async-start | bytes 1179648 | tf_op jit(solution)/shard_map/all_gather | solution.py:240
  304.1 89.0 %all-gather.12.cloned.1.call-start = ((), (), s32[]{:S(2)}) async-start(), calls=%async_computation.17 | async-start | bytes 2621440 | tf_op jit(solution)/shard_map/all_gather | solution.py:60
  312.5 233.6 %copy-start.78 = (f32[8,1,128]{2,1,0:T(1,128)}, f32[8,1,128]{2,1,0:T(1,128)S(1)}, u32[]{:S(2)}) copy-start(f32[8,1,128]{2,1,0:T(1,128)S(1)} %convert_element_type.363) | copy-start | bytes 12292
  346.1 200.0 %copy-start.92 = (f32[256]{0:T(256)}, f32[256]{0:T(256)S(1)}, u32[]{:S(2)}) copy-start(f32[256]{0:T(256)S(1)} %add_rsqrt_fusion.1) | copy-start | bytes 3076
  348.2 69.1 %all-gather.16.cloned.1.call-start = ((), (), s32[]{:S(2)}) async-start(), calls=%async_computation.19 | async-start | bytes 1179648 | tf_op jit(solution)/shard_map/all_gather | solution.py:241
  348.7 94.0 %all-gather.18.cloned.1.call-start = ((), (), s32[]{:S(2)}) async-start(), calls=%async_computation.20 | async-start | bytes 1179648 | tf_op jit(solution)/shard_map/all_gather | solution.py:244
  349.5 140.5 %all-gather.20.cloned.1.call-start = ((), (), s32[]{:S(2)}) async-start(), calls=%async_computation.22 | async-start | bytes 2621440 | tf_op jit(solution)/shard_map/all_gather | solution.py:60
  350.2 193.6 %reduce-scatter.20.cloned.1.call-start = ((), (), s32[]{:S(2)}) async-start(), calls=%async_computation.23 | async-start | bytes 2621440 | tf_op jit(solution)/shard_map/reduce_scatter | solution.py:64
  500.9 42.9 %copy-start.9 = (bf16[256,1024]{1,0:T(8,128)(2,1)S(1)}, bf16[256,1024]{1,0:T(8,128)(2,1)}, u32[]{:S(2)}) copy-start(bf16[256,1024]{1,0:T(8,128)(2,1)} %reduce-scatter.16.cloned.1.call-done) | copy-start | bytes 1572868
  501.0 91.8 %all-gather.22.cloned.1.call-start = ((), (), s32[]{:S(2)}) async-start(), calls=%async_computation.24 | async-start | bytes 2621440 | tf_op jit(solution)/shard_map/all_gather | solution.py:60
  547.3 47.9 %copy-start.60 = (bf16[1024,2,64]{0,1,2:T(2,128)(2,1)S(1)}, bf16[1024,2,64]{0,1,2:T(2,128)(2,1)}, u32[]{:S(2)}) copy-start(bf16[1024,2,64]{0,1,2:T(2,128)(2,1)} %fusion.133) | copy-start | bytes 786436
  547.4 756.6 %reduce-scatter.34.cloned.1.call-start = ((), (), s32[]{:S(2)}) async-start(), calls=%async_computation.31 | async-start | bytes 1179648 | tf_op jit(solution)/shard_map/reduce_scatter | solution.py:388
  1256.7 73.6 %reduce-scatter.26.cloned.1.call-start = ((), (), s32[]{:S(2)}) async-start(), calls=%async_computation.27 | async-start | bytes 1179648 | tf_op jit(solution)/shard_map/reduce_scatter | solution.py:385
  1285.2 97.0 %all-reduce.34.cloned.1.call-start = ((), (), s32[]{:S(2)}) async-start(), calls=%async_computation.37 | async-start | bytes 262144 | tf_op jit(solution)/shard_map/psum | solution.py:415
  1331.8 80.6 %reduce-scatter.22.cloned.1.call-start = ((), (), s32[]{:S(2)}) async-start(), calls=%async_computation.25 | async-start | bytes 2621440 | tf_op jit(solution)/shard_map/reduce_scatter | solution.py:64
  1343.8 114.4 %reduce-scatter.18.cloned.1.call-start = ((), (), s32[]{:S(2)}) async-start(), calls=%async_computation.21 | async-start | bytes 2621440 | tf_op jit(solution)/shard_map/reduce_scatter | solution.py:64
  1348.1 154.9 %reduce-scatter.40.cloned.1.call-start = ((), (), s32[]{:S(2)}) async-start(), calls=%async_computation.34 | async-start | bytes 2359296 | tf_op jit(solution)/shard_map/reduce_scatter | solution.py:393
  1352.6 195.5 %reduce-scatter.42.cloned.1.call-start = ((), (), s32[]{:S(2)}) async-start(), calls=%async_computation.35 | async-start | bytes 2359296 | tf_op jit(solution)/shard_map/reduce_scatter | solution.py:394
  1357.2 236.2 %reduce-scatter.44.cloned.1.call-start = ((), (), s32[]{:S(2)}) async-start(), calls=%async_computation.36 | async-start | bytes 2359296 | tf_op jit(solution)/shard_map/reduce_scatter | solution.py:395
  1361.8 266.5 %reduce-scatter.36.cloned.1.call-start = ((), (), s32[]{:S(2)}) async-start(), calls=%async_computation.32 | async-start | bytes 36864 | tf_op jit(solution)/shard_map/reduce_scatter | solution.py:389
  1363.5 302.8 %reduce-scatter.24.cloned.1.call-start = ((), (), s32[]{:S(2)}) async-start(), calls=%async_computation.26 | async-start | bytes 589824 | tf_op jit(solution)/shard_map/reduce_scatter | solution.py:384
  1366.1 337.9 %reduce-scatter.28.cloned.1.call-start = ((), (), s32[]{:S(2)}) async-start(), calls=%async_computation.28 | async-start | bytes 589824 | tf_op jit(solution)/shard_map/reduce_scatter | solution.py:390
  1369.1 377.5 %reduce-scatter.38.cloned.1.call-start = ((), (), s32[]{:S(2)}) async-start(), calls=%async_computation.33 | async-start | bytes 1769472 | tf_op jit(solution)/shard_map/reduce_scatter | solution.py:391
  1373.5 415.7 %reduce-scatter.32.cloned.1.call-start = ((), (), s32[]{:S(2)}) async-start(), calls=%async_computation.30 | async-start | bytes 1769472 | tf_op jit(solution)/shard_map/reduce_scatter | solution.py:387
  1377.3 454.4 %reduce-scatter.30.cloned.1.call-start = ((), (), s32[]{:S(2)}) async-start(), calls=%async_computation.29 | async-start | bytes 1769472 | tf_op jit(solution)/shard_map/reduce_scatter | solution.py:386
  1380.2 32.2 %copy-start.86 = (f32[8,1,128]{2,1,0:T(1,128)S(1)}, f32[8,1,128]{2,1,0:T(1,128)}, u32[]{:S(2)}) copy-start(f32[8,1,128]{2,1,0:T(1,128)} %copy-done.85) | copy-start | bytes 12292
  1380.2 32.2 %copy-start.107 = (f32[256]{0:T(256)S(1)}, f32[256]{0:T(256)}, u32[]{:S(2)}) copy-start(f32[256]{0:T(256)} %copy-done.106) | copy-start | bytes 3076
  1380.2 33.7 %copy-start.102 = (f32[6]{0:T(128)S(1)}, f32[6]{0:T(128)}, u32[]{:S(2)}) copy-start(f32[6]{0:T(128)} %get-tuple-element.735) | copy-start | bytes 76
  1380.2 33.7 %copy-start.105 = (f32[1024]{0:T(1024)S(1)}, f32[1024]{0:T(1024)}, u32[]{:S(2)}) copy-start(f32[1024]{0:T(1024)} %get-tuple-element.1075) | copy-start | bytes 12292
  1380.2 33.7 %copy-start.131 = (f32[256]{0:T(256)S(1)}, f32[256]{0:T(256)}, u32[]{:S(2)}) copy-start(f32[256]{0:T(256)} %get-tuple-element.1081) | copy-start | bytes 3076
  1380.2 33.7 %copy-start.139 = (f32[6]{0:T(128)S(1)}, f32[6]{0:T(128)}, u32[]{:S(2)}) copy-start(f32[6]{0:T(128)} %get-tuple-element.1191) | copy-start | bytes 76
  1380.2 33.7 %copy-start.141 = (f32[384]{0:T(512)S(1)}, f32[384]{0:T(512)}, u32[]{:S(2)}) copy-start(f32[384]{0:T(512)} %get-tuple-element.1067) | copy-start | bytes 4612
  1380.3 77.9 %copy-start.10 = (bf16[256,1024]{1,0:T(8,128)(2,1)S(1)}, bf16[256,1024]{1,0:T(8,128)(2,1)}, u32[]{:S(2)}) copy-start(bf16[256,1024]{1,0:T(8,128)(2,1)} %reduce-scatter.16.cloned.1.call-done) | copy-start | bytes 1572868
  1380.3 77.9 %copy-start.22 = (bf16[256,1024]{1,0:T(8,128)(2,1)S(1)}, bf16[256,1024]{1,0:T(8,128)(2,1)}, u32[]{:S(2)}) copy-start(bf16[256,1024]{1,0:T(8,128)(2,1)} %param.31) | copy-start | bytes 1572868
  1380.3 77.9 %copy-start.24 = (bf16[256,1024]{1,0:T(8,128)(2,1)S(1)}, bf16[256,1024]{1,0:T(8,128)(2,1)}, u32[]{:S(2)}) copy-start(bf16[256,1024]{1,0:T(8,128)(2,1)} %reduce-scatter.20.cloned.1.call-done) | copy-start | bytes 1572868
  1380.3 77.9 %copy-start.79 = (f32[8,1,128]{2,1,0:T(1,128)S(1)}, f32[8,1,128]{2,1,0:T(1,128)}, u32[]{:S(2)}) copy-start(f32[8,1,128]{2,1,0:T(1,128)} %copy-done.78) | copy-start | bytes 12292
  1380.3 77.9 %copy-start.93 = (f32[256]{0:T(256)S(1)}, f32[256]{0:T(256)}, u32[]{:S(2)}) copy-start(f32[256]{0:T(256)} %copy-done.92) | copy-start | bytes 3076
  1380.3 77.9 %copy-start.115 = (f32[256]{0:T(256)S(1)}, f32[256]{0:T(256)}, u32[]{:S(2)}) copy-start(f32[256]{0:T(256)} %copy-done.114) | copy-start | bytes 3076
  (190 other events, 1004.3 us)
Sparse Core Ops, SparseCore 0:
  22.0 46.1 all-gather.9
  303.7 41.0 reduce-scatter.15
  501.1 42.6 reduce-scatter.19
  547.5 45.2 all-gather.21
  1331.9 34.5 all-reduce.33
  1368.8 43.5 reduce-scatter.21
  1414.7 43.4 reduce-scatter.17
  1462.4 40.5 reduce-scatter.39
  1506.8 41.2 reduce-scatter.41
  1552.1 41.2 reduce-scatter.43
  1597.0 31.2 reduce-scatter.35
  1632.1 34.1 reduce-scatter.23
  1669.9 34.0 reduce-scatter.27
  1708.1 38.4 reduce-scatter.37
  1750.7 38.4 reduce-scatter.31
  1793.2 38.4 reduce-scatter.29
Sparse Core Ops, SparseCore 1:
  306.1 20.5 all-gather.13
  348.2 44.9 all-gather.11
  395.1 22.1 all-gather.15
  419.3 23.4 all-gather.17
  444.4 45.5 all-gather.19
  1256.8 34.4 reduce-scatter.33
  1294.3 35.9 reduce-scatter.25
where the time goes:
time: 1860 us; the launch traced here: 1840 us
  waiting for transfers between devices  682 us (37%)
  local copies, waits for them, and re-layouts  434 us (23%)
  matrix products  308 us (17%)
  other arithmetic  206 us (11%)
  blocking collectives  155 us (8%)
  loops' own time  34.2 us (2%)
    dynamic_update_slice x32, local copies, waits for them, and re-layouts, ssd_core(): unused, outputs = lax.scan(jax.checkpoint(one_block), initial, pieces)  156 us
    all_gather x4, waiting for transfers between devices, gather_rows(): return lax.all_gather(values, 'tensor', axis=0, tiled=True)  135 us
    reduce_scatter x4, waiting for transfers between devices, sum_rows(): lax.psum_scatter(values.astype(jnp.bfloat16), 'tensor', scatter_dimension...  108 us
    squeeze x88, local copies, waits for them, and re-layouts, ssd_core(): unused, outputs = lax.scan(jax.checkpoint(one_block), initial, pieces)  82.8 us
    dot_general x32, matrix products, one_block(): within = jnp.einsum('ijh,jhp->ihp', mixing, x_blk, precision=HIGHEST)  55.8 us
    dot_general x40, matrix products, one_block(): jnp.dot(c_blk, b_blk.T, precision=HIGHEST, preferred_element_type=jnp.flo...  52.9 us
    reduce_scatter x1, waiting for transfers between devices, local(): lax.psum_scatter(grad_down, 'dp', scatter_dimension=1, tiled=True)  45.3 us
    another operation x40, other arithmetic, one_block(): cumlog = jnp.cumsum(logdecay_blk, axis=0)  45.2 us
  transfers between devices with their start and end apart: 23, of which 19 were waited for; matrix products, arithmetic and copies ran while one was open for 7% of the time, Pallas kernels for 0%

commit v1 on v0

v1 whole, which is shorter than its diff:
```python
import math

import jax
import jax.numpy as jnp
import numpy as np
from jax import lax
from jax.experimental import pallas as pl
from jax.experimental.pallas import tpu as pltpu
from jax.sharding import PartitionSpec as P

QH = 8
KVH = 2
HD = 64
MH = 24
PD = 64
NS = 128
KW = 4
BLOCK = 128
LANES = 128

EPSILON = 1e-05
ROPE_BASE = 100000000000.0
NEG = -1e9
F32 = jnp.float32
BF16 = jnp.bfloat16
VMEM_LIMIT = 48 * 1024 * 1024


def mm(lhs, rhs):
    return lax.dot_general(lhs, rhs, (((1,), (0,)), ((), ())), preferred_element_type=F32)


def mm_nt(lhs, rhs):
    return lax.dot_general(lhs, rhs, (((1,), (1,)), ((), ())), preferred_element_type=F32)


def mm_tn(lhs, rhs):
    return lax.dot_general(lhs, rhs, (((0,), (0,)), ((), ())), preferred_element_type=F32)


def rms_scale(values):
    return lax.rsqrt(jnp.mean(values * values, axis=-1, keepdims=True) + EPSILON)


def norm_back(grad_normed, normed, scale):
    return scale * (grad_normed - normed * jnp.mean(grad_normed * normed, axis=-1, keepdims=True))


def sigmoid(v):
    return 1.0 / (1.0 + jnp.exp(-v))


def iota(shape, dim):
    return lax.broadcasted_iota(jnp.int32, shape, dim)


def rope_tables(length):
    half = HD // 2
    freqs = np.float32(ROPE_BASE) ** (-(np.arange(half, dtype=np.float32) * np.float32(2.0 / HD)))
    angles = np.arange(length, dtype=np.float32)[:, None] * freqs.astype(np.float32)[None, :]
    cosine, sine = np.cos(angles).astype(np.float32), np.sin(angles).astype(np.float32)
    cos_lanes = np.concatenate([cosine] * 4, axis=1)
    sin_lanes = np.concatenate([-sine, sine, -sine, sine], axis=1)
    return jnp.asarray(cos_lanes), jnp.asarray(sin_lanes)


def swap_halves(values):
    lane = iota(values.shape, 1)
    ahead = pltpu.roll(values, LANES - HD // 2, 1)
    behind = pltpu.roll(values, HD // 2, 1)
    return jnp.where((lane & (HD - 1)) < HD // 2, ahead, behind)


def pair_rows(block):
    low = iota(block.shape, 1) < HD
    zero = jnp.zeros_like(block)
    return jnp.concatenate([jnp.where(low, block, zero), jnp.where(low, zero, block)], axis=0)


def attn_fwd_kernel(q_ref, kv_ref, cos_ref, sin_ref, start_ref, out_ref, lse_ref, lq_ref, lkv_ref):
    length = q_ref.shape[0]
    rows = 256
    cosine, sine = cos_ref[...], sin_ref[...]
    low = iota((length, LANES), 1) < HD
    queries = q_ref[...]
    lq_ref[...] = (queries * cosine + swap_halves(queries) * sine).astype(BF16)
    kv = kv_ref[...]
    kv = jnp.where(low, kv * cosine + swap_halves(kv) * sine, kv)
    lkv_ref[...] = kv.astype(BF16)
    other = pltpu.roll(kv, HD, 1)
    keys = jnp.where(low, kv, other).astype(BF16)
    vals = jnp.where(low, other, kv).astype(BF16)
    half = iota((rows, LANES), 1) < HD
    for step in range(length // rows):
        end = (step + 1) * rows
        span = slice(step * rows, end)
        stacked = pair_rows(lq_ref[span, :].astype(F32)).astype(BF16)
        scores = mm_nt(stacked, keys[:end]) * (1.0 / math.sqrt(HD))
        first = start_ref[span, :][:, :1]
        col = iota((rows, end), 1)
        row = iota((rows, end), 0) + step * rows
        allowed = (col <= row) & (col >= first)
        allowed = jnp.concatenate([allowed.astype(jnp.int32)] * 2, axis=0) > 0
        scores = jnp.where(allowed, scores, NEG)
        top = jnp.max(scores, axis=1, keepdims=True)
        expo = jnp.exp(scores - top)
        total = jnp.sum(expo, axis=1, keepdims=True)
        probs = (expo * (1.0 / total)).astype(BF16)
        result = mm(probs, vals[:end])
        out_ref[span, :] = jnp.where(half, result[:rows], result[rows:]).astype(BF16)
        lse = top + jnp.log(total)
        lse_ref[span, :] = jnp.where(half, lse[:rows], lse[rows:])


def attn_bwd_kernel(
    lq_ref, lkv_ref, lse_ref, out_ref, go_ref, cos_ref, sin_ref, start_ref, gq_ref, gkv_ref, dk_ref, dv_ref
):
    length = lq_ref.shape[0]
    rows = 256
    cosine, sine = cos_ref[...], sin_ref[...]
    low = iota((length, LANES), 1) < HD
    kv = lkv_ref[...].astype(F32)
    other = pltpu.roll(kv, HD, 1)
    keys = jnp.where(low, kv, other).astype(BF16)
    vals = jnp.where(low, other, kv).astype(BF16)
    half = iota((rows, LANES), 1) < HD
    dk_ref[...] = jnp.zeros_like(dk_ref)
    dv_ref[...] = jnp.zeros_like(dv_ref)
    inv = 1.0 / math.sqrt(HD)
    for step in range(length // rows):
        end = (step + 1) * rows
        span = slice(step * rows, end)
        stacked = pair_rows(lq_ref[span, :].astype(F32)).astype(BF16)
        grads = pair_rows(go_ref[span, :].astype(F32))
        outs = out_ref[span, :].astype(F32)
        inner = jnp.sum(grads * jnp.concatenate([outs, outs], axis=0), axis=1, keepdims=True)
        grads = grads.astype(BF16)
        lse = lse_ref[span, :]
        lse = jnp.concatenate([lse[:, :1], lse[:, HD : HD + 1]], axis=0)
        scores = mm_nt(stacked, keys[:end]) * inv
        first = start_ref[span, :][:, :1]
        col = iota((rows, end), 1)
        row = iota((rows, end), 0) + step * rows
        allowed = (col <= row) & (col >= first)
        allowed = jnp.concatenate([allowed.astype(jnp.int32)] * 2, axis=0) > 0
        probs = jnp.exp(jnp.where(allowed, scores, NEG) - lse)
        grad_probs = mm_nt(grads, vals[:end])
        grad_scores = (probs * (grad_probs - inner)).astype(BF16)
        gq = mm(grad_scores, keys[:end]) * inv
        gq = jnp.where(half, gq[:rows], gq[rows:])
        gq_ref[span, :] = (gq * cosine[span] - swap_halves(gq) * sine[span]).astype(BF16)
        dk_ref[:end, :] += mm_tn(grad_scores, stacked)
        dv_ref[:end, :] += mm_tn(probs.astype(BF16), grads)
    dk = dk_ref[...] * inv
    dk = dk + pltpu.roll(dk, HD, 1)
    dk = dk * cosine - swap_halves(dk) * sine
    dv = dv_ref[...]
    dv = dv + pltpu.roll(dv, HD, 1)
    gkv_ref[...] = jnp.where(low, dk, dv).astype(BF16)


def attn_forward(proj, cosine, sine, start_col):
    length = proj.shape[0]
    wide = pl.BlockSpec((length, LANES), lambda i: (0, 0))
    return pl.pallas_call(
        attn_fwd_kernel,
        grid=(1,),
        in_specs=[wide, pl.BlockSpec((length, LANES), lambda i: (0, 1)), wide, wide, wide],
        out_specs=[wide] * 4,
        out_shape=[
            jax.ShapeDtypeStruct((length, LANES), BF16),
            jax.ShapeDtypeStruct((length, LANES), F32),
            jax.ShapeDtypeStruct((length, LANES), BF16),
            jax.ShapeDtypeStruct((length, LANES), BF16),
        ],
        compiler_params=pltpu.CompilerParams(vmem_limit_bytes=VMEM_LIMIT),
        cost_estimate=pl.CostEstimate(flops=10**9, bytes_accessed=6 * 10**6, transcendentals=2 * 10**6),
        name="attn_fwd",
    )(proj, proj, cosine, sine, start_col)


def attn_backward(low_q, low_kv, lse, out, grad_out, cosine, sine, start_col):
    length = low_q.shape[0]
    wide = pl.BlockSpec((length, LANES), lambda i: (0, 0))
    return pl.pallas_call(
        attn_bwd_kernel,
        grid=(1,),
        in_specs=[wide] * 8,
        out_specs=[wide] * 2,
        out_shape=[jax.ShapeDtypeStruct((length, LANES), BF16)] * 2,
        scratch_shapes=[pltpu.VMEM((length, LANES), F32)] * 2,
        compiler_params=pltpu.CompilerParams(vmem_limit_bytes=VMEM_LIMIT),
        cost_estimate=pl.CostEstimate(flops=3 * 10**9, bytes_accessed=6 * 10**6, transcendentals=2 * 10**6),
        name="attn_bwd",
    )(low_q, low_kv, lse, out, grad_out, cosine, sine, start_col)


def split3(values):
    high = values.astype(BF16).astype(F32)
    rest = values - high
    mid = rest.astype(BF16).astype(F32)
    tail = rest - mid
    return jnp.concatenate([high, mid, tail, jnp.zeros_like(values)], axis=0).astype(BF16)


def spread(rows, width, lanes_each):
    pick = (iota((32, width), 1) // lanes_each) == (iota((32, width), 0) & 7)
    return mm_tn(split3(rows), pick.astype(F32).astype(BF16))


def decay_terms(dt_block, dt_bias, rate, start_row, start_col, base):
    dt_rows = jnp.transpose(dt_block)[:8] + dt_bias
    step = jnp.maximum(dt_rows, 0.0) + jnp.log1p(jnp.exp(-jnp.abs(dt_rows)))
    log_decay = -step * rate
    row = iota((BLOCK, BLOCK), 0) + base
    col = iota((BLOCK, BLOCK), 1) + base
    linked = (col <= row) & (col >= start_col)
    linked_low = jnp.where(linked, 1.0, 0.0).astype(BF16)
    cum = mm_nt(split3(log_decay), linked_low)
    cum = cum[0:8] + cum[8:16] + cum[16:24]
    enter = jnp.exp(jnp.where(start_row < base, cum, NEG))
    last = cum[:, BLOCK - 1 :]
    position = iota((8, BLOCK), 1) + base
    tail = jnp.exp(jnp.where(position >= start_row[:, BLOCK - 1 :], last - cum, NEG))
    return dt_rows, step, log_decay, linked, linked_low, cum, enter, tail


def conv_sum(ext_ref, taps, bias, place):
    total = bias + taps[KW - 1 : KW] * ext_ref[pl.ds(8, BLOCK), :]
    for offset in range(1, KW):
        shifted = ext_ref[pl.ds(8 - offset, BLOCK), :]
        total = total + jnp.where(place >= offset, taps[KW - 1 - offset : KW - offset] * shifted, 0.0)
    return total


def wide_place(start_col, base, width):
    place = iota((BLOCK, BLOCK), 0) + base - start_col
    return jnp.concatenate([place] * (width // LANES), axis=1)


def scan_fwd_kernel(
    cols,
    proj_ref,
    startc_ref,
    startr_ref,
    taps_ref,
    bias_ref,
    dtb_ref,
    rate_ref,
    skip_ref,
    y_ref,
    gated_ref,
    state_out_ref,
    ssq_ref,
    state_ref,
    ext_ref,
):
    zat, xat, dat, width = cols
    channels = xat - zat
    heads = channels // PD
    block = pl.program_id(0)
    base = block * BLOCK

    @pl.when(block == 0)
    def _():
        state_ref[...] = jnp.zeros_like(state_ref)
        ext_ref[0:8, :] = jnp.zeros((8, ext_ref.shape[1]), F32)

    start_col = startc_ref[...]
    start_row = startr_ref[...]
    ext_ref[pl.ds(8, BLOCK), :] = proj_ref[:, xat:dat]
    place = wide_place(start_col, base, dat - xat)
    pre = conv_sum(ext_ref, taps_ref[...], bias_ref[...], place)
    ext_ref[0:8, :] = ext_ref[pl.ds(BLOCK, 8), :]
    conv = (pre * sigmoid(pre)).astype(BF16)
    x_low, b_low, c_low = conv[:, :channels], conv[:, channels : channels + NS], conv[:, channels + NS :]
    x_val = x_low.astype(F32)
    _, step, _, linked, _, cum, enter, tail = decay_terms(
        proj_ref[:, dat:width], dtb_ref[...], rate_ref[...], start_row, start_col, base
    )
    contact = mm_nt(c_low, b_low)
    cum_cols = spread(cum, heads * LANES, LANES)
    enter_x = spread(enter, channels, PD)
    weight_x = spread(tail * step, channels, PD)
    low = iota((BLOCK, LANES), 1) < PD
    zero = jnp.zeros((BLOCK, LANES), F32)
    within = []
    for pair in range(heads // 2):
        mixes = []
        for head in (2 * pair, 2 * pair + 1):
            gap = cum_cols[:, head * LANES : (head + 1) * LANES] - cum[head : head + 1]
            decay = jnp.exp(jnp.where(linked, gap, NEG))
            mixes.append((decay * (contact * step[head : head + 1])).astype(BF16))
        x_pair = x_val[:, pair * LANES : (pair + 1) * LANES]
        both = jnp.concatenate([jnp.where(low, x_pair, zero), jnp.where(low, zero, x_pair)], axis=0).astype(BF16)
        within.append(mm(jnp.concatenate(mixes, axis=1), both))
    state = state_ref[...]
    state_low = state.astype(BF16)
    state_out_ref[0] = state_low
    y = jnp.concatenate(within, axis=1) + enter_x * mm(c_low, state_low) + skip_ref[...] * x_val
    y_ref[...] = y
    state_ref[...] = mm_tn(b_low, (weight_x * x_val).astype(BF16)) + enter_x[BLOCK - 1 :] * state
    z = proj_ref[:, zat:xat]
    gated = y * (z * sigmoid(z))
    gated_ref[...] = gated
    square = gated * gated
    high = square.astype(BF16)
    rest = (square - high.astype(F32)).astype(BF16)
    ones = jnp.ones((16, channels), BF16)
    ssq_ref[...] = (mm_nt(ones, high) + mm_nt(ones, rest))[:8]


def scan_bwd_kernel(
    cols,
    proj_ref,
    prev_ref,
    startc_ref,
    startr_ref,
    taps_ref,
    bias_ref,
    dtb_ref,
    rate_ref,
    skip_ref,
    y_ref,
    state_in_ref,
    grad_ref,
    out_ref,
    conv_acc_ref,
    head_acc_ref,
    skip_acc_ref,
    dstate_ref,
    ext_ref,
    dext_ref,
    pext_ref,
):
    zat, xat, dat, width = cols
    channels = xat - zat
    heads = channels // PD
    turn = pl.program_id(0)
    block = pl.num_programs(0) - 1 - turn
    base = block * BLOCK

    @pl.when(turn == 0)
    def _():
        dstate_ref[...] = jnp.zeros_like(dstate_ref)
        conv_acc_ref[...] = jnp.zeros_like(conv_acc_ref)
        head_acc_ref[...] = jnp.zeros_like(head_acc_ref)
        skip_acc_ref[...] = jnp.zeros_like(skip_acc_ref)
        dext_ref[pl.ds(BLOCK, 8), :] = jnp.zeros((8, dext_ref.shape[1]), F32)
        pext_ref[pl.ds(BLOCK, 8), :] = jnp.zeros((8, LANES), jnp.int32)

    start_col = startc_ref[...]
    start_row = startr_ref[...]
    taps = taps_ref[...]
    ext_ref[0:8, :] = prev_ref[:, xat:dat]
    ext_ref[pl.ds(8, BLOCK), :] = proj_ref[:, xat:dat]
    place = wide_place(start_col, base, dat - xat)
    pre = conv_sum(ext_ref, taps, bias_ref[...], place)
    pre_sig = sigmoid(pre)
    conv = (pre * pre_sig).astype(BF16)
    x_low, b_low, c_low = conv[:, :channels], conv[:, channels : channels + NS], conv[:, channels + NS :]
    x_val = x_low.astype(F32)
    rate = rate_ref[...]
    dt_rows, step, log_decay, linked, linked_low, cum, enter, tail = decay_terms(
        proj_ref[:, dat:width], dtb_ref[...], rate, start_row, start_col, base
    )
    contact = mm_nt(c_low, b_low)
    cum_cols = spread(cum, heads * LANES, LANES)
    enter_x = spread(enter, channels, PD)
    weight = tail * step
    weight_x = spread(weight, channels, PD)

    z = proj_ref[:, zat:xat]
    z_sig = sigmoid(z)
    grad = grad_ref[...]
    dy = grad * (z * z_sig)
    out_ref[:, : channels] = (grad * y_ref[...] * (z_sig * (1.0 + z * (1.0 - z_sig)))).astype(BF16)

    low = iota((BLOCK, LANES), 1) < PD
    strict = linked & (iota((BLOCK, BLOCK), 0) > iota((BLOCK, BLOCK), 1))
    zero = jnp.zeros((BLOCK, LANES), F32)
    dcontact = zero
    dx_parts, w_parts, step_rows = [], [], []
    for pair in range(heads // 2):
        lanes = slice(pair * LANES, (pair + 1) * LANES)
        dy_pair = dy[:, lanes]
        dy_both = jnp.concatenate([jnp.where(low, dy_pair, zero), jnp.where(low, zero, dy_pair)], axis=0).astype(BF16)
        outer = mm_nt(dy_both, x_low[:, lanes])
        mixes = []
        for slot in range(2):
            head = 2 * pair + slot
            gap = cum_cols[:, head * LANES : (head + 1) * LANES] - cum[head : head + 1]
            decay = jnp.exp(jnp.where(linked, gap, NEG))
            step_row = step[head : head + 1]
            share = outer[slot * BLOCK : (slot + 1) * BLOCK] * decay
            dcontact = dcontact + share * step_row
            flow = share * contact
            step_rows.append(jnp.sum(flow, axis=0, keepdims=True))
            w_parts.append(jnp.where(strict, flow * step_row, 0.0).astype(BF16))
            mixes.append((decay * (contact * step_row)).astype(BF16))
        dx_parts.append(mm_tn(jnp.concatenate(mixes, axis=0), dy_both))
    pad = [jnp.zeros((8 - heads, BLOCK), F32)] if heads < 8 else []
    dstep = jnp.concatenate(step_rows + pad, axis=0)
    pick_rows = (iota((16, heads * BLOCK), 1) // BLOCK) == iota((16, heads * BLOCK), 0)
    pick_rows = jnp.where(pick_rows, 1.0, 0.0).astype(BF16)
    dcum = mm_nt(pick_rows, jnp.concatenate(w_parts, axis=1))[:8]
    dcum = dcum - mm(pick_rows, jnp.concatenate(w_parts, axis=0))[:8]

    state_low = state_in_ref[0]
    dstate = dstate_ref[...]
    dstate_low = dstate.astype(BF16)
    pick_x = (iota((16, channels), 1) // PD) == iota((16, channels), 0)
    pick_f = jnp.where(pick_x, 1.0, 0.0)
    pick_x = pick_f.astype(BF16)
    from_state = enter_x * mm(c_low, state_low)
    dcum = dcum + mm_nt(pick_x, (dy * from_state).astype(BF16))[:8]
    dye = (enter_x * dy).astype(BF16)
    through = mm(b_low, dstate_low)
    dweight = mm_nt(pick_x, (x_val * through).astype(BF16))[:8]
    wx = (weight_x * x_val).astype(BF16)
    kept_x = enter_x[BLOCK - 1 :]
    dkept = jnp.sum(dstate * state_low.astype(F32), axis=0, keepdims=True) * kept_x
    dkept = jnp.sum(pick_f[:8] * dkept, axis=1, keepdims=True)
    moved = dweight * weight
    lane = iota((8, BLOCK), 1)
    dlast = jnp.sum(moved, axis=1, keepdims=True) + dkept
    dcum = dcum - moved + jnp.where(lane == BLOCK - 1, dlast, 0.0)
    dstep = dstep + dweight * tail
    dc = mm_nt(dye, state_low)
    db = mm_nt(wx, dstate_low)
    dstate_ref[...] = mm_tn(c_low, dye) + kept_x * dstate
    dcontact_low = dcontact.astype(BF16)
    dc = dc + mm(dcontact_low, b_low)
    db = db + mm_tn(dcontact_low, c_low)
    dx = jnp.concatenate(dx_parts, axis=1) + weight_x * through + skip_ref[...] * dy

    dlog = mm(split3(dcum), linked_low)
    dlog = dlog[0:8] + dlog[8:16] + dlog[16:24]
    dstep = dstep - dlog * rate
    ddt = dstep * sigmoid(dt_rows)
    head_acc_ref[0:8, :] += ddt
    head_acc_ref[8:16, :] += dlog * log_decay
    skip_acc_ref[0:1, :] += jnp.sum(dy * x_val, axis=0, keepdims=True)
    ddt_cols = jnp.transpose(jnp.concatenate([ddt, jnp.zeros((BLOCK - 8, BLOCK), F32)], axis=0))
    out_ref[:, dat - zat : width - zat] = ddt_cols.astype(BF16)

    dpre = jnp.concatenate([dx, db, dc], axis=1) * (pre_sig * (1.0 + pre * (1.0 - pre_sig)))
    conv_acc_ref[KW : KW + 1, :] += jnp.sum(dpre, axis=0, keepdims=True)
    dext_ref[0:BLOCK, :] = dpre
    pext_ref[0:BLOCK, :] = iota((BLOCK, BLOCK), 0) + base - start_col
    draw = taps[KW - 1 : KW] * dpre
    conv_acc_ref[KW - 1 : KW, :] += jnp.sum(dpre * ext_ref[pl.ds(8, BLOCK), :], axis=0, keepdims=True)
    for offset in range(1, KW):
        tap = KW - 1 - offset
        kept = jnp.where(place >= offset, dpre * ext_ref[pl.ds(8 - offset, BLOCK), :], 0.0)
        conv_acc_ref[tap : tap + 1, :] += jnp.sum(kept, axis=0, keepdims=True)
        later = pext_ref[pl.ds(offset, BLOCK), :]
        later = jnp.concatenate([later] * ((dat - xat) // LANES), axis=1)
        draw = draw + jnp.where(later >= offset, taps[tap : tap + 1] * dext_ref[pl.ds(offset, BLOCK), :], 0.0)
    dext_ref[pl.ds(BLOCK, 8), :] = dext_ref[0:8, :]
    pext_ref[pl.ds(BLOCK, 8), :] = pext_ref[0:8, :]
    out_ref[:, xat - zat : dat - zat] = draw.astype(BF16)


def scan_specs(cols, turn):
    zat, xat, dat, width = cols
    channels = xat - zat
    conv_width = dat - xat
    fixed = lambda shape: pl.BlockSpec(shape, lambda c: (0,) * len(shape))
    params = [
        fixed((8, conv_width)),
        fixed((1, conv_width)),
        fixed((8, LANES)),
        fixed((8, LANES)),
        fixed((1, channels)),
    ]
    starts = [
        pl.BlockSpec((BLOCK, LANES), lambda c: (turn(c), 0)),
        pl.BlockSpec((8, BLOCK), lambda c: (0, turn(c))),
    ]
    return starts, params


def scan_forward(cols, proj, start_col, start_row, params):
    zat, xat, dat, width = cols
    channels = xat - zat
    length = proj.shape[0]
    blocks = length // BLOCK
    starts, param_specs = scan_specs(cols, lambda c: c)
    body = lambda *refs: scan_fwd_kernel(cols, *refs)
    return pl.pallas_call(
        body,
        grid=(blocks,),
        in_specs=[pl.BlockSpec((BLOCK, width), lambda c: (c, 0))] + starts + param_specs,
        out_specs=[
            pl.BlockSpec((BLOCK, channels), lambda c: (c, 0)),
            pl.BlockSpec((BLOCK, channels), lambda c: (c, 0)),
            pl.BlockSpec((1, NS, channels), lambda c: (c, 0, 0)),
            pl.BlockSpec((8, BLOCK), lambda c: (0, c)),
        ],
        out_shape=[
            jax.ShapeDtypeStruct((length, channels), F32),
            jax.ShapeDtypeStruct((length, channels), F32),
            jax.ShapeDtypeStruct((blocks, NS, channels), BF16),
            jax.ShapeDtypeStruct((8, length), F32),
        ],
        scratch_shapes=[
            pltpu.VMEM((NS, channels), F32),
            pltpu.VMEM((BLOCK + 8, dat - xat), F32),
        ],
        compiler_params=pltpu.CompilerParams(vmem_limit_bytes=VMEM_LIMIT),
        cost_estimate=pl.CostEstimate(flops=2 * 10**9, bytes_accessed=10**7, transcendentals=2 * 10**6),
        name="scan_fwd",
    )(proj, start_col, start_row, *params)


def scan_backward(cols, proj, start_col, start_row, params, y, states, grad):
    zat, xat, dat, width = cols
    channels = xat - zat
    length = proj.shape[0]
    blocks = length // BLOCK
    turn = lambda c: blocks - 1 - c
    starts, param_specs = scan_specs(cols, turn)
    body = lambda *refs: scan_bwd_kernel(cols, *refs)
    tall = BLOCK // 8
    return pl.pallas_call(
        body,
        grid=(blocks,),
        in_specs=[
            pl.BlockSpec((BLOCK, width), lambda c: (turn(c), 0)),
            pl.BlockSpec((8, width), lambda c: (jnp.maximum(turn(c) * tall - 1, 0), 0)),
        ]
        + starts
        + param_specs
        + [
            pl.BlockSpec((BLOCK, channels), lambda c: (turn(c), 0)),
            pl.BlockSpec((1, NS, channels), lambda c: (turn(c), 0, 0)),
            pl.BlockSpec((BLOCK, channels), lambda c: (turn(c), 0)),
        ],
        out_specs=[
            pl.BlockSpec((BLOCK, width - zat), lambda c: (turn(c), 0)),
            pl.BlockSpec((8, dat - xat), lambda c: (0, 0)),
            pl.BlockSpec((16, LANES), lambda c: (0, 0)),
            pl.BlockSpec((8, channels), lambda c: (0, 0)),
        ],
        out_shape=[
            jax.ShapeDtypeStruct((length, width - zat), BF16),
            jax.ShapeDtypeStruct((8, dat - xat), F32),
            jax.ShapeDtypeStruct((16, LANES), F32),
            jax.ShapeDtypeStruct((8, channels), F32),
        ],
        scratch_shapes=[
            pltpu.VMEM((NS, channels), F32),
            pltpu.VMEM((BLOCK + 8, dat - xat), F32),
            pltpu.VMEM((BLOCK + 8, dat - xat), F32),
            pltpu.VMEM((BLOCK + 8, LANES), jnp.int32),
        ],
        compiler_params=pltpu.CompilerParams(vmem_limit_bytes=VMEM_LIMIT),
        cost_estimate=pl.CostEstimate(flops=6 * 10**9, bytes_accessed=2 * 10**7, transcendentals=3 * 10**6),
        name="scan_bwd",
    )(proj, proj, start_col, start_row, *params, y, states, grad)


def pack_kernel(cols, place_ref, q_ref, kv_ref, z_ref, x_ref, bc_ref, dt_ref, norms_ref, att_ref, mix_ref, gate_ref, up_ref, down_ref, mixer_ref, ffn_ref):
    zat, xat, dat, width = cols
    own = q_ref.shape[0]
    qwidth = q_ref.shape[1]
    channels = xat - zat
    hidden = gate_ref.shape[1]
    eye = jnp.where(iota((own, own), 0) == iota((own, own), 1), 1.0, 0.0).astype(BF16)
    turned = lambda ref: mm_nt(eye, ref[...]).astype(BF16)
    mixer_ref[:, :qwidth] = q_ref[...]
    kv = kv_ref[...].astype(F32)
    keys, vals = kv[:, :LANES], kv[:, LANES:]
    first = place_ref[0] == 0
    keys = jnp.where(first, keys, pltpu.roll(keys, HD, 1))
    vals = jnp.where(first, pltpu.roll(vals, HD, 1), vals)
    mixer_ref[:, qwidth:zat] = jnp.where(iota((own, LANES), 1) < HD, keys, vals).astype(BF16)
    mixer_ref[:, zat:xat] = z_ref[...]
    mixer_ref[:, xat : xat + channels] = x_ref[...]
    mixer_ref[:, xat + channels : dat] = bc_ref[...]
    mixer_ref[:, dat:width] = turned(norms_ref)
    mixer_ref[:, dat : dat + dt_ref.shape[1]] = dt_ref[...]
    mixer_ref[:, width : width + qwidth] = turned(att_ref)
    mixer_ref[:, width + qwidth :] = turned(mix_ref)
    ffn_ref[:, :hidden] = gate_ref[...]
    ffn_ref[:, hidden : 2 * hidden] = up_ref[...]
    ffn_ref[:, 2 * hidden :] = turned(down_ref)


def pack_weights(cols, kv_head, *shards):
    own = shards[0].shape[0]
    zat, xat, dat, width = cols
    body = lambda *refs: pack_kernel(cols, *refs)
    whole = pl.BlockSpec(memory_space=pltpu.VMEM)
    return pl.pallas_call(
        body,
        in_specs=[pl.BlockSpec(memory_space=pltpu.SMEM)] + [whole] * len(shards),
        out_specs=[whole] * 2,
        out_shape=[
            jax.ShapeDtypeStruct((own, width + shards[0].shape[1] + xat - zat), BF16),
            jax.ShapeDtypeStruct((own, 3 * shards[-1].shape[0]), BF16),
        ],
        compiler_params=pltpu.CompilerParams(vmem_limit_bytes=VMEM_LIMIT),
        cost_estimate=pl.CostEstimate(flops=10**7, bytes_accessed=2 * 10**6, transcendentals=0),
        name="pack_weights",
    )(kv_head, *shards)


def norm_kernel(parts, rank_ref, *refs):
    gain_ref, out_ref = refs[parts], refs[parts + 1]
    rows = refs[0].shape[0]
    gain = gain_ref[...]
    for shift in range(parts):
        values = refs[shift][...].astype(F32)
        spot = lax.rem(rank_ref[0] + (parts - shift), parts) * rows
        out_ref[pl.ds(pl.multiple_of(spot, rows), rows), :] = (values * rms_scale(values) * gain).astype(BF16)


def norm_rows(rank, pieces, gain):
    parts = len(pieces)
    rows, model = pieces[0].shape
    body = lambda *refs: norm_kernel(parts, *refs)
    whole = pl.BlockSpec(memory_space=pltpu.VMEM)
    return pl.pallas_call(
        body,
        in_specs=[pl.BlockSpec(memory_space=pltpu.SMEM)] + [whole] * (parts + 1),
        out_specs=whole,
        out_shape=jax.ShapeDtypeStruct((parts * rows, model), BF16),
        compiler_params=pltpu.CompilerParams(vmem_limit_bytes=VMEM_LIMIT),
        cost_estimate=pl.CostEstimate(flops=10**7, bytes_accessed=4 * 10**6, transcendentals=0),
        name="norm_rows",
    )(rank, *pieces, gain)


def ffn_kernel(middle_ref, cot_ref, gain_ref, w_ref, out_ref, gmid_ref, ggain_ref, gw_ref, low_ref, sum_ref, gsum_ref):
    step = pl.program_id(0)
    hidden = w_ref.shape[1] // 3

    @pl.when(step == 0)
    def _():
        middle = middle_ref[...]
        low_ref[...] = (middle * rms_scale(middle) * gain_ref[...]).astype(BF16)
        sum_ref[...] = jnp.zeros_like(sum_ref)
        gsum_ref[...] = jnp.zeros_like(gsum_ref)

    low = low_ref[...]
    cot = cot_ref[...]
    gate_pre = mm(low, w_ref[:, :hidden])
    up_pre = mm(low, w_ref[:, hidden : 2 * hidden])
    sig = sigmoid(gate_pre)
    silu_gate = gate_pre * sig
    act = (silu_gate * up_pre).astype(BF16)
    sum_ref[...] += mm_nt(act, w_ref[:, 2 * hidden :])
    gw_ref[:, 2 * hidden :] = mm_tn(cot, act).astype(BF16)
    grad_hidden = mm(cot, w_ref[:, 2 * hidden :])
    grad_gate = (grad_hidden * up_pre * sig * (1.0 + gate_pre * (1.0 - sig))).astype(BF16)
    grad_up = (grad_hidden * silu_gate).astype(BF16)
    gw_ref[:, :hidden] = mm_tn(low, grad_gate).astype(BF16)
    gw_ref[:, hidden : 2 * hidden] = mm_tn(low, grad_up).astype(BF16)
    gsum_ref[...] += mm_nt(grad_gate, w_ref[:, :hidden]) + mm_nt(grad_up, w_ref[:, hidden : 2 * hidden])

    @pl.when(step == pl.num_programs(0) - 1)
    def _():
        middle = middle_ref[...]
        out_ref[...] = (middle + sum_ref[...]).astype(BF16)
        scale = rms_scale(middle)
        normed = middle * scale
        grad_two = gsum_ref[...]
        ggain_ref[...] = jnp.broadcast_to(jnp.sum(grad_two * normed, axis=0, keepdims=True), ggain_ref.shape)
        gmid_ref[...] = cot_ref[...].astype(F32) + norm_back(grad_two * gain_ref[...], normed, scale)


def ffn_both(middle, cotangent, gain, ffn_w, parts):
    rows, model = middle.shape
    piece = ffn_w.shape[1] // parts
    rowspec = pl.BlockSpec((rows, model), lambda s: (0, 0))
    wspec = pl.BlockSpec((model, piece), lambda s: (0, s))
    return pl.pallas_call(
        ffn_kernel,
        grid=(parts,),
        in_specs=[rowspec, rowspec, pl.BlockSpec((1, model), lambda s: (0, 0)), wspec],
        out_specs=[rowspec, rowspec, pl.BlockSpec((8, model), lambda s: (0, 0)), wspec],
        out_shape=[
            jax.ShapeDtypeStruct((rows, model), BF16),
            jax.ShapeDtypeStruct((rows, model), F32),
            jax.ShapeDtypeStruct((8, model), F32),
            jax.ShapeDtypeStruct(ffn_w.shape, BF16),
        ],
        scratch_shapes=[
            pltpu.VMEM((rows, model), BF16),
            pltpu.VMEM((rows, model), F32),
            pltpu.VMEM((rows, model), F32),
        ],
        compiler_params=pltpu.CompilerParams(vmem_limit_bytes=VMEM_LIMIT),
        cost_estimate=pl.CostEstimate(flops=10**10, bytes_accessed=3 * 10**7, transcendentals=10**6),
        name="ffn_both",
    )(middle, cotangent, gain, ffn_w)


def lane_rows(values, rows):
    padded = jnp.pad(values, (0, rows - values.shape[0]))
    return jnp.broadcast_to(padded[:, None], (rows, LANES))


def shifted(values, axis, size, shift):
    return lax.ppermute(values, axis, [(i, (i + shift) % size) for i in range(size)])


def pieces_of_group(values, parts):
    return [values] + [shifted(values, "tensor", parts, shift) for shift in range(1, parts)]


def in_order(pieces, rank):
    parts, rows = len(pieces), pieces[0].shape[0]
    line = jnp.concatenate(pieces[:0:-1] + pieces[:1] + pieces[:0:-1], axis=0)
    return lax.dynamic_slice(line, ((parts - 1 - rank) * rows, 0), (parts * rows, line.shape[1]))


def rows_of(values, rank, shift, parts):
    rows = values.shape[0] // parts
    return lax.dynamic_slice(values, (lax.rem(rank + shift, parts) * rows, 0), (rows, values.shape[1]))


def group_total(values, parts):
    total = values.astype(F32)
    for shift in range(1, parts):
        total = total + shifted(values, "tensor", parts, shift).astype(F32)
    return total


def butterfly(values, axis, size):
    if size & (size - 1):
        return lax.psum(values, axis)
    step = 1
    while step < size:
        values = values + lax.ppermute(values, axis, [(i, i ^ step) for i in range(size)])
        step *= 2
    return values


def local(
    x_in,
    cotangent,
    segments,
    norm_one,
    w_query,
    w_keyval,
    w_attn_out,
    w_zgate,
    w_xin,
    w_bcin,
    w_dtin,
    conv_x,
    conv_bc,
    bias_x,
    bias_bc,
    dt_bias,
    a_log,
    d_skip,
    ssm_gain,
    w_mix_out,
    norm_two,
    w_gate,
    w_up,
    w_down,
):
    parts = lax.axis_size("tensor")
    rank = lax.axis_index("tensor")
    own = w_query.shape[0]
    length = segments.shape[1]
    qwidth = w_query.shape[1]
    channels = w_zgate.shape[1]
    heads = w_dtin.shape[1]
    hidden_own = w_gate.shape[1]
    width_ssm = MH * PD
    kv_head = (rank * (qwidth // HD)) // (QH // KVH)
    zat = 2 * qwidth
    xat = zat + channels
    bat = xat + channels
    dat = bat + 2 * NS
    width = dat + LANES
    cols = (zat, xat, dat, width)

    norms = jnp.zeros((LANES, own), BF16).at[HD].set(norm_one).at[HD + 1].set(norm_two)
    x_pieces = pieces_of_group(x_in, parts)
    mixer_own, ffn_own = pack_weights(
        cols,
        kv_head.astype(jnp.int32)[None],
        w_query,
        w_keyval,
        w_zgate,
        w_xin,
        w_bcin,
        w_dtin,
        norms,
        w_attn_out,
        w_mix_out,
        w_gate,
        w_up,
        w_down,
    )
    mixer_w = lax.all_gather(mixer_own, "dp", axis=0, tiled=True)
    proj_w = mixer_w[:, :width]
    out_w = mixer_w[:, width:]
    gain_one = mixer_w[:, dat + HD].astype(F32)[None, :]
    gain_two = mixer_w[:, dat + HD + 1].astype(F32)[None, :]
    ffn_own = jnp.concatenate(pieces_of_group(ffn_own, parts), axis=1)
    ffn_w = lax.all_gather(ffn_own, "dp", axis=0, tiled=True)

    seg = segments[0]
    start = jnp.sum((seg[None, :] < seg[:, None]).astype(jnp.int32), axis=1)
    start_col = jnp.broadcast_to(start[:, None], (length, LANES))
    start_row = jnp.broadcast_to(start[None, :], (8, length))
    cosine, sine = rope_tables(length)
    taps = jnp.pad(jnp.concatenate([conv_x, conv_bc], axis=1), ((0, 8 - KW), (0, 0)))
    bias = jnp.concatenate([bias_x, bias_bc])[None, :]
    params = (taps, bias, lane_rows(dt_bias, 8), lane_rows(jnp.exp(a_log), 8), jnp.repeat(d_skip, PD)[None, :])

    residual = x_in.astype(F32)
    scale_one = rms_scale(residual)
    normed_one = residual * scale_one
    rows_one = norm_rows(rank.astype(jnp.int32)[None], x_pieces, gain_one)
    proj = mm(rows_one, proj_w)
    y, gated, states, squares = scan_forward(cols, proj, start_col, start_row, params)
    attended, lse, low_q, low_kv = attn_forward(proj, cosine, sine, start_col)
    scale_ssm = lax.rsqrt(group_total(squares[:1], parts)[0] / width_ssm + EPSILON)[:, None]
    normed_ssm = gated * scale_ssm
    mixed = (normed_ssm * ssm_gain[None, :]).astype(BF16)
    att_mixed = jnp.concatenate([attended, mixed], axis=1)
    middle = residual
    for shift in range(parts):
        term = mm_nt(rows_of(att_mixed, rank, shift, parts), out_w)
        middle = middle + (shifted(term.astype(BF16), "tensor", parts, shift).astype(F32) if shift else term)
    block_out, grad_middle, grad_gain_two, grad_ffn_w = ffn_both(middle, cotangent, gain_two, ffn_w, parts)

    grad_branch = in_order(pieces_of_group(grad_middle.astype(BF16), parts), rank)
    grad_ffn_own = lax.psum_scatter(grad_ffn_w, "dp", scatter_dimension=0, tiled=True)
    piece = grad_ffn_own.shape[1] // parts
    grad_ffn = 0.0
    for shift in range(parts):
        term = grad_ffn_own[:, shift * piece : (shift + 1) * piece]
        grad_ffn = grad_ffn + (shifted(term, "tensor", parts, -shift) if shift else term).astype(F32)
    grad_am = mm(grad_branch, out_w)
    grad_att = grad_am[:, :qwidth].astype(BF16)
    grad_mixed = grad_am[:, qwidth:]
    grad_out_w = mm_tn(grad_branch, att_mixed)
    grad_gain_ssm = jnp.sum(grad_mixed * normed_ssm, axis=0)
    grad_normed = grad_mixed * ssm_gain[None, :]
    row_inner = group_total(jnp.sum(grad_normed * normed_ssm, axis=-1)[None, :], parts)[0]
    grad_gated = scale_ssm * (grad_normed - normed_ssm * (row_inner / width_ssm)[:, None])
    grad_q, grad_kv = attn_backward(low_q, low_kv, lse, attended, grad_att, cosine, sine, start_col)
    grad_rest, conv_acc, head_acc, skip_acc = scan_backward(
        cols, proj, start_col, start_row, params, y, states, grad_gated
    )
    grad_proj = jnp.concatenate([grad_q, grad_kv, grad_rest], axis=1)
    grad_one, grad_gain_one = 0.0, 0.0
    for shift in range(parts):
        term = mm_nt(rows_of(grad_proj, rank, shift, parts), proj_w)
        grad_gain_one = grad_gain_one + jnp.sum(
            term * rows_of(rows_one, rank, shift, parts).astype(F32), axis=0, keepdims=True
        )
        grad_one = grad_one + (shifted(term.astype(BF16), "tensor", parts, shift).astype(F32) if shift else term)
    grad_gain_one = grad_gain_one / gain_one
    grad_input = grad_middle + norm_back(grad_one * gain_one, normed_one, scale_one)
    grad_mixer_w = jnp.concatenate([mm_tn(rows_one, grad_proj), grad_out_w], axis=1).astype(BF16)
    grad_w = lax.psum_scatter(grad_mixer_w, "dp", scatter_dimension=0, tiled=True).astype(F32)

    model = x_in.shape[1]
    wide = lambda rows: jnp.pad(rows, ((0, 0), (0, model - rows.shape[1])))
    head_sums = jnp.sum(head_acc, axis=1)[None, :]
    small = jnp.concatenate(
        [
            wide(conv_acc),
            grad_gain_one,
            grad_gain_two[:1],
            wide(grad_gain_ssm[None, :]),
            wide(skip_acc[:1]),
            wide(head_sums),
            jnp.zeros((3, model), F32),
        ],
        axis=0,
    )
    small = butterfly(small, "dp", lax.axis_size("dp"))
    shared_small = butterfly(small, "tensor", parts)
    grad_conv_x = small[:KW, :channels]
    grad_bias_x = small[KW, :channels]
    grad_ssm_gain = small[10, :channels]
    grad_d_skip = jnp.sum(small[11, :channels].reshape(heads, PD), axis=1)
    grad_dt_bias = small[12, :heads]
    grad_a_log = small[12, 8 : 8 + heads]
    grad_conv_bc = shared_small[:KW, channels : channels + 2 * NS]
    grad_bias_bc = shared_small[KW, channels : channels + 2 * NS]
    place = lax.axis_index("dp") * own
    norm_grads = lax.dynamic_slice(shared_small, (8, place), (2, own))
    grad_norm_one, grad_norm_two = norm_grads[0], norm_grads[1]

    grad_keyval = jnp.zeros((own, 2 * KVH * HD), F32)
    grad_keyval = lax.dynamic_update_slice(grad_keyval, grad_w[:, qwidth : qwidth + HD], (0, kv_head * HD))
    grad_keyval = lax.dynamic_update_slice(
        grad_keyval, grad_w[:, qwidth + HD : zat], (0, (KVH + kv_head) * HD)
    )
    shared = jnp.concatenate([grad_keyval, grad_w[:, bat:dat]], axis=1)
    shared = group_total(shared.astype(BF16), parts)

    return (
        block_out,
        grad_input,
        grad_norm_one,
        grad_w[:, :qwidth],
        shared[:, : 2 * KVH * HD],
        grad_w[:, width : width + qwidth].T,
        grad_w[:, zat:xat],
        grad_w[:, xat:bat],
        shared[:, 2 * KVH * HD :],
        grad_w[:, dat : dat + heads],
        grad_conv_x,
        grad_conv_bc,
        grad_bias_x,
        grad_bias_bc,
        grad_dt_bias,
        grad_a_log,
        grad_d_skip,
        grad_ssm_gain,
        grad_w[:, width + qwidth :].T,
        grad_norm_two,
        grad_ffn[:, :hidden_own],
        grad_ffn[:, hidden_own : 2 * hidden_own],
        grad_ffn[:, 2 * hidden_own :].T,
    )


def solution(mesh):
    return jax.shard_map(
        local,
        mesh=mesh,
        in_specs=(
            P(("dp", "tensor"), None),
            P(("dp", "tensor"), None),
            P("dp", None),
            P("dp"),
            P("dp", "tensor"),
            P("dp", None),
            P("tensor", "dp"),
            P("dp", "tensor"),
            P("dp", "tensor"),
            P("dp", None),
            P("dp", "tensor"),
            P(None, "tensor"),
            P(),
            P("tensor"),
            P(),
            P("tensor"),
            P("tensor"),
            P("tensor"),
            P("tensor"),
            P("tensor", "dp"),
            P("dp"),
            P("dp", "tensor"),
            P("dp", "tensor"),
            P("tensor", "dp"),
        ),
        out_specs=(
            P(("dp", "tensor"), None),
            P(("dp", "tensor"), None),
            P("dp"),
            P("dp", "tensor"),
            P("dp", None),
            P("tensor", "dp"),
            P("dp", "tensor"),
            P("dp", "tensor"),
            P("dp", None),
            P("dp", "tensor"),
            P(None, "tensor"),
            P(),
            P("tensor"),
            P(),
            P("tensor"),
            P("tensor"),
            P("tensor"),
            P("tensor"),
            P("tensor", "dp"),
            P("dp"),
            P("dp", "tensor"),
            P("dp", "tensor"),
            P("tensor", "dp"),
        ),
        check_vma=False,
    )
```

time: 1860 us -> 515 us (0.28)
  waiting for transfers between devices: 682 us -> 252 us
  local copies, waits for them, and re-layouts: 434 us -> 39.1 us
  matrix products: 308 us -> 36.6 us
  other arithmetic: 206 us -> 14.2 us
  blocking collectives: 155 us -> 0 us
  starting transfers between devices: 1.97 us -> 89.4 us
  Pallas kernels: 0 us -> 59.6 us
  loops' own time: 34.2 us -> 0 us
    reduce_scatter x15 -> x2, waiting for transfers between devices: 503 us -> 54.9 us  [the longest x1 54.9 us: local(): lax.psum_scatter(grad_ffn_w, 'dp', scatter_dimension=0, tiled=True)]
    dot_general x187 -> x12, matrix products: 308 us -> 36.6 us  [the longest x8 23.8 us: mm_nt(): lax.dot_general(lhs, rhs, (((1,), (1,)), ((), ())), preferred_element_typ...]
    ppermute x0 -> x32, waiting for transfers between devices: none -> 197 us  [the longest x27 188 us: shifted(): lax.ppermute(values, axis, [(i, (i + shift) % size) for i in range(size)])]
    all_gather x7 -> x2, waiting for transfers between devices: 176 us -> 0.02 us  [the longest x1 0.02 us: local(): mixer_w = lax.all_gather(mixer_own, 'dp', axis=0, tiled=True)]
    dynamic_update_slice x32 -> x2, local copies, waits for them, and re-layouts: 156 us -> 0.43 us  [the longest x1 0.23 us: local(): lax.dynamic_update_slice(grad_keyval, grad_w[:, qwidth:qwidth + HD], (0,...]
    all_gather x10 -> x0, blocking collectives: 97.8 us -> none  [the longest x1 11.1 us: local(): lax.all_gather(w_mix_out, 'dp', axis=1, tiled=True)]
    ppermute x0 -> x32, starting transfers between devices: none -> 89 us  [the longest x27 77.5 us: shifted(): lax.ppermute(values, axis, [(i, (i + shift) % size) for i in range(size)])]
    squeeze x88 -> x2, local copies, waits for them, and re-layouts: 82.8 us -> 1.1 us  [the longest x1 0.58 us: local(): grad_a_log = small[12, 8:8 + heads]]
  transfers between devices with their start and end apart: 23 -> 36, of which waited for: 19 -> 19; matrix products, arithmetic and copies ran while one was open for 7% -> 10% of each run, Pallas kernels for 0% -> 5%
where the time goes in v1:
time: 515 us; the launch traced here: 506 us
  waiting for transfers between devices  252 us (49%)
  starting transfers between devices  89.4 us (17%)
  Pallas kernels  59.6 us (12%)
  local copies, waits for them, and re-layouts  39.1 us (8%)
  matrix products  36.6 us (7%)
  between operations  15.1 us (3%)
  other arithmetic  14.2 us (3%)
    ppermute x27, waiting for transfers between devices, shifted(): lax.ppermute(values, axis, [(i, (i + shift) % size) for i in range(size)])  188 us
    ppermute x27, starting transfers between devices, shifted(): lax.ppermute(values, axis, [(i, (i + shift) % size) for i in range(size)])  77.5 us
    reduce_scatter x1, waiting for transfers between devices, local(): lax.psum_scatter(grad_ffn_w, 'dp', scatter_dimension=0, tiled=True)  54.9 us
    dot_general x8, matrix products, mm_nt(): lax.dot_general(lhs, rhs, (((1,), (1,)), ((), ())), preferred_element_typ...  23.8 us
    unnamed x108, local copies, waits for them, and re-layouts  23.7 us
    pallas_call x1, Pallas kernels, scan_backward(): pl.pallas_call(body, grid=(blocks,), in_specs=[pl.BlockSpec((BLOCK, width...  19.3 us
    pallas_call x1, Pallas kernels, ffn_both(): pl.pallas_call(ffn_kernel, grid=(parts,), in_specs=[rowspec, rowspec, pl....  16.5 us
    ppermute x5, starting transfers between devices, butterfly(): lax.ppermute(values, axis, [(i, i ^ step) for i in range(size)])  11.5 us
  transfers between devices with their start and end apart: 36, of which 19 were waited for; matrix products, arithmetic and copies ran while one was open for 10% of the time, Pallas kernels for 5%

profile of v1, /device:TPU:0, one launch (start us, length us, event | category | flops | bytes accessed | tf_op | source)
XLA Modules:
  0.0 505.8 jit_solution(2699790892621804215)
XLA Ops:
  19.1 4.1 collective-permute-start.10
  23.2 1.3 collective-permute-start.11
  25.3 17.3 %collective-permute-done.10 = bf16[128,1536]{1,0:T(8,128)(2,1)S(1)} collective-permute-done((bf16[128,1536]{1,0:T(8,128)(2,1)S(1)}, bf16[128,1536]{1,0:T(8,128)(2,1)S(1)}, u32[]{:S(2)}, u32[]{:S(2)}) %collective-permute-start.10) | collective-permute-done | bytes 393248 | tf_op jit(solution)/shard_map/ppermute | solution.py:707
  42.5 7.9 %collective-permute-done.9 = bf16[128,1536]{1,0:T(8,128)(2,1)S(1)} collective-permute-done((bf16[128,1536]{1,0:T(8,128)(2,1)S(1)}, bf16[128,1536]{1,0:T(8,128)(2,1)S(1)}, u32[]{:S(2)}, u32[]{:S(2)}) %collective-permute-start.9) | collective-permute-done | bytes 393248 | tf_op jit(solution)/shard_map/ppermute | solution.py:707
  50.4 1.3 pad_maximum_fusion.2
  51.8 19.1 %collective-permute-start = (bf16[256,1024]{1,0:T(8,128)(2,1)S(1)}, bf16[256,1024]{1,0:T(8,128)(2,1)S(1)}, u32[]{:S(2)}, u32[]{:S(2)}) collective-permute-start(bf16[256,1024]{1,0:T(8,128)(2,1)S(1)} %copy-done), channel_id=1, source_target_pairs={{0,1},{1,2},{2,3},{3,0},{4,5},{5,6},{6,7},{7,4},{8,9},{9,10},{10,1... | collective-permute-start | bytes 1572872 | tf_op jit(solution)/shard_map/ppermute | solution.py:707
  71.0 2.4 collective-permute-start.2
  74.3 1.6 convert_reduce_fusion.1
  75.9 7.4 %collective-permute-done.refs_2_ = bf16[256,1024]{1,0:T(8,128)(2,1)S(1)} collective-permute-done((bf16[256,1024]{1,0:T(8,128)(2,1)S(1)}, bf16[256,1024]{1,0:T(8,128)(2,1)S(1)}, u32[]{:S(2)}, u32[]{:S(2)}) %collective-permute-start) | collective-permute-done | bytes 524320 | tf_op jit(solution)/shard_map/ppermute | solution.py:707
  83.3 12.5 %collective-permute-done.1.refs_3_ = bf16[256,1024]{1,0:T(8,128)(2,1)S(1)} collective-permute-done((bf16[256,1024]{1,0:T(8,128)(2,1)S(1)}, bf16[256,1024]{1,0:T(8,128)(2,1)S(1)}, u32[]{:S(2)}, u32[]{:S(2)}) %collective-permute-start.1) | collective-permute-done | bytes 524320 | tf_op jit(solution)/shard_map/ppermute | solution.py:707
  95.8 8.3 %collective-permute-done.2.refs_4_ = bf16[256,1024]{1,0:T(8,128)(2,1)S(1)} collective-permute-done((bf16[256,1024]{1,0:T(8,128)(2,1)S(1)}, bf16[256,1024]{1,0:T(8,128)(2,1)S(1)}, u32[]{:S(2)}, u32[]{:S(2)}) %collective-permute-start.2) | collective-permute-done | bytes 524320 | tf_op jit(solution)/shard_map/ppermute | solution.py:707
  104.9 5.2 %fusion.12.q_ref.kv_ref.refs_0_.refs_1_ = f32[1024,1408]{1,0:T(8,128)} fusion(bf16[1024,1024]{1,0:T(8,128)(2,1)S(1)} %norm_rows.1, bf16[1024,1920]{1,0:T(8,128)(2,1)S(1)} %copy-done.33), kind=kOutput, calls=%fused_computation.28 | convolution fusion | flops 2952790016 | bytes 10747904 | tf_op jit(solution)/shard_map/dot_general | solution.py:30
  110.5 9.9 %scan_fwd.1 = (f32[1024,384]{1,0:T(8,128)S(1)}, f32[1024,384]{1,0:T(8,128)S(1)}, bf16[8,128,384]{2,1,0:T(8,128)(2,1)S(1)}, f32[8,1024]{1,0:T(8,128)S(1)}) custom-call(f32[1024,1408]{1,0:T(8,128)} %fusion.12.q_ref.kv_ref.refs_0_.refs_1_, s32[1024,128]{1,0:T(8,128)S(1)} %broadcast_in_dim.28.start_ref.refs_1_.refs_2_, ...), custom_call_target="tpu_custom_call" | custom-call | flops 2000000000 | bytes 10000000 | tf_op jit(solution)/shard_map/scan_fwd/pallas_call | solution.py:491
  120.4 1.2 copy-done.27
  121.5 11.4 %collective-permute-start.3 = (f32[1,1024]{1,0:T(1,128)S(1)}, f32[1,1024]{1,0:T(1,128)S(1)}, u32[]{:S(2)}, u32[]{:S(2)}) collective-permute-start(f32[1,1024]{1,0:T(1,128)S(1)} %slice.144), channel_id=1, source_target_pairs={{0,1},{1,2},{2,3},{3,0},{4,5},{5,6},{6,7},{7,4},{8,9},{9,10},{10,1... | collective-permute-start | bytes 12296 | tf_op jit(solution)/shard_map/ppermute | solution.py:707
  132.9 3.4 collective-permute-start.4
  136.3 5.6 %attn_fwd.1 = (bf16[1024,128]{1,0:T(8,128)(2,1)S(1)}, f32[1024,128]{1,0:T(8,128)S(1)}, bf16[1024,128]{1,0:T(8,128)(2,1)S(1)}, bf16[1024,128]{1,0:T(8,128)(2,1)S(1)}) custom-call(f32[1024,1408]{1,0:T(8,128)} %fusion.12.q_ref.kv_ref.refs_0_.refs_1_, f32[1024,1408]{1,0:T(8,128)} %fusion.12.q_ref.kv_ref.refs_0_.refs_1_, f32[1024,128]{1,0:T(8,128)S(1)} %copy-done.6, ...), custom_call_target="tpu_custom_call" | custom-call | flops 1000000000 | bytes 6000000 | tf_op jit(solution)/shard_map/attn_fwd/pallas_call | solution.py:165
  142.2 1.3 convolution_convert_fusion.3
  143.5 2.0 collective-permute-start.6
  145.5 1.3 convolution_convert_fusion.2
  146.9 1.3 convolution_convert_fusion.1
  148.2 2.6 collective-permute-start.8
  150.8 9.9 %collective-permute-done.6 = bf16[256,1024]{1,0:T(8,128)(2,1)} collective-permute-done((bf16[256,1024]{1,0:T(8,128)(2,1)}, bf16[256,1024]{1,0:T(8,128)(2,1)}, u32[]{:S(2)}, u32[]{:S(2)}) %collective-permute-start.6) | collective-permute-done | bytes 524320 | tf_op jit(solution)/shard_map/ppermute | solution.py:707
  160.7 19.6 %collective-permute-done.7 = bf16[256,1024]{1,0:T(8,128)(2,1)} collective-permute-done((bf16[256,1024]{1,0:T(8,128)(2,1)}, bf16[256,1024]{1,0:T(8,128)(2,1)}, u32[]{:S(2)}, u32[]{:S(2)}) %collective-permute-start.7) | collective-permute-done | bytes 524320 | tf_op jit(solution)/shard_map/ppermute | solution.py:707
  180.2 3.3 convert_add_fusion.1.middle_ref
  183.5 1.2 copy-done.5
  185.8 16.5 %ffn_both.1 = (bf16[256,1024]{1,0:T(8,128)(2,1)}, f32[256,1024]{1,0:T(8,128)S(1)}, f32[8,1024]{1,0:T(8,128)S(1)}, bf16[1024,6144]{1,0:T(8,128)(2,1)}) custom-call(f32[256,1024]{1,0:T(8,128)S(1)} %copy-done.5, bf16[256,1024]{1,0:T(8,128)(2,1)S(1)} %copy-done.20, f32[1,1024]{1,0:T(1,128)S(1)} %bitcast.32, bf16[1024,6144]{1,0:T(8,128)(2,1)} %all-gather.5.cloned.1.call-done.w_ref), custom_call_target="tpu_custom_call" | custom-call | flops 10000000000 | bytes 30000000 | tf_op jit(solution)/shard_map/ffn_both/pallas_call | solution.py:679
  203.1 11.7 %collective-permute-start.12 = (bf16[256,1024]{1,0:T(8,128)(2,1)}, bf16[256,1024]{1,0:T(8,128)(2,1)}, u32[]{:S(2)}, u32[]{:S(2)}) collective-permute-start(bf16[256,1024]{1,0:T(8,128)(2,1)} %convert_element_type.151), channel_id=1, source_target_pairs={{0,3},{1,0},{2,1},{3,2},{4,7},{5,4},{6,5},{7,6},{8,11},{9,8},{10,9... | collective-permute-start | bytes 1572872 | tf_op jit(solution)/shard_map/ppermute | solution.py:707
  214.8 1.5 collective-permute-start.13
  216.3 11.3 %collective-permute-done.12 = bf16[256,1024]{1,0:T(8,128)(2,1)} collective-permute-done((bf16[256,1024]{1,0:T(8,128)(2,1)}, bf16[256,1024]{1,0:T(8,128)(2,1)}, u32[]{:S(2)}, u32[]{:S(2)}) %collective-permute-start.12) | collective-permute-done | bytes 524320 | tf_op jit(solution)/shard_map/ppermute | solution.py:707
  228.6 33.5 %collective-permute-done.13 = bf16[256,1024]{1,0:T(8,128)(2,1)} collective-permute-done((bf16[256,1024]{1,0:T(8,128)(2,1)}, bf16[256,1024]{1,0:T(8,128)(2,1)}, u32[]{:S(2)}, u32[]{:S(2)}) %collective-permute-start.13) | collective-permute-done | bytes 524320 | tf_op jit(solution)/shard_map/ppermute | solution.py:707
  263.2 1.1 constant_dynamic-update-slice_fusion.4
  267.7 1.3 fusion.14
  269.0 2.5 fusion.2
  272.3 3.9 collective-permute-start.17
  276.3 6.6 %attn_bwd.1 = (bf16[1024,128]{1,0:T(8,128)(2,1)S(1)}, bf16[1024,128]{1,0:T(8,128)(2,1)S(1)}) custom-call(bf16[1024,128]{1,0:T(8,128)(2,1)S(1)} %copy-done.24, bf16[1024,128]{1,0:T(8,128)(2,1)S(1)} %copy-done.26, f32[1024,128]{1,0:T(8,128)S(1)} %copy-done.22, bf16[1024,128]{1,0:T(8,128)(2,1)S(1)} %get-tuple-element.68.out_ref, ...), custom_call_target="tpu_custom_call" | custom-call | flops 3000000000 | bytes 6000000 | tf_op jit(solution)/shard_map/attn_bwd/pallas_call | solution.py:185
  284.5 19.3 %scan_bwd.1 = (bf16[1024,1152]{1,0:T(8,128)(2,1)}, f32[8,640]{1,0:T(8,128)S(1)}, f32[16,128]{1,0:T(8,128)S(1)}, f32[8,384]{1,0:T(8,128)S(1)}) custom-call(f32[1024,1408]{1,0:T(8,128)} %fusion.12.q_ref.kv_ref.refs_0_.refs_1_, f32[1024,1408]{1,0:T(8,128)} %fusion.12.q_ref.kv_ref.refs_0_.refs_1_, s32[1024,128]{1,0:T(8,128)S(1)} %copy-done.4, ...), custom_call_target="tpu_custom_call" | custom-call | flops 6000000000 | bytes 20000000 | tf_op jit(solution)/shard_map/scan_bwd/pallas_call | solution.py:526
  303.8 2.2 constant_dynamic-update-slice_fusion.7
  306.1 3.7 convolution_convert_fusion
  309.9 2.2 pad_maximum_fusion
  312.6 4.4 fusion.63
  317.0 2.0 collective-permute-start.19
  319.0 3.4 fusion.62
  323.3 3.3 fusion.64
  326.7 1.1 collective-permute-start.18
  328.2 16.2 %collective-permute-done.19 = bf16[256,1024]{1,0:T(8,128)(2,1)S(1)} collective-permute-done((bf16[256,1024]{1,0:T(8,128)(2,1)}, bf16[256,1024]{1,0:T(8,128)(2,1)S(1)}, u32[]{:S(2)}, u32[]{:S(2)}) %collective-permute-start.19) | collective-permute-done | bytes 524320 | tf_op jit(solution)/shard_map/ppermute | solution.py:707
  344.3 12.5 %collective-permute-done.20 = bf16[256,1024]{1,0:T(8,128)(2,1)S(1)} collective-permute-done((bf16[256,1024]{1,0:T(8,128)(2,1)}, bf16[256,1024]{1,0:T(8,128)(2,1)S(1)}, u32[]{:S(2)}, u32[]{:S(2)}) %collective-permute-start.20) | collective-permute-done | bytes 524320 | tf_op jit(solution)/shard_map/ppermute | solution.py:707
  357.8 5.6 %multiply_reduce_fusion.4 = (f32[1024]{0:T(1024)S(1)}, f32[1024]{0:T(1024)S(1)}, f32[1024]{0:T(1024)S(1)}, f32[1024]{0:T(1024)S(1)}, f32[256]{0:T(256)S(1)}, /*index=5*/f32[256,1024]{1,0:T(8,128)S(1)}) fusion(f32[256,1024]{1,0:T(8,128)} %get-tuple-element.189, bf16[1024,1024]{1,0:T(8,128)(2,1)} %copy-done.1, s32[]{:T(128)S(6)} %select_n.39, ...), kind=kOutput, calls=%fused_computation.48 | convolution fusion | flops 744222464 | bytes 12018176 | tf_op jit(solution)/shard_map/dot_general | solution.py:34
  363.5 1.2 collective-permute-done.21
  364.8 1.1 collective-permute-start.22
  365.9 3.2 collective-permute-done.22
  370.2 2.9 fusion.22
  373.5 8.1 %collective-permute-start.24 = (f32[16,1024]{1,0:T(8,128)S(1)}, f32[16,1024]{1,0:T(8,128)S(1)}, u32[]{:S(2)}, u32[]{:S(2)}) collective-permute-start(f32[16,1024]{1,0:T(8,128)S(1)} %add.242), channel_id=1, source_target_pairs={{0,1},{1,0},{2,3},{3,2},{4,5},{5,4},{6,7},{7,6},{8,9},{9,8},{10,11... | collective-permute-start | bytes 196616 | tf_op jit(solution)/shard_map/ppermute | solution.py:737
  386.2 2.8 collective-permute-done.25
  393.1 2.3 collective-permute-start.26
  395.3 1.1 collective-permute-start.27
  396.5 1.3 collective-permute-start.28
  402.5 54.9 %reduce-scatter.5.cloned.1.call-done = bf16[128,6144]{1,0:T(8,128)(2,1)} async-done(((bf16[1024,6144]{1,0:T(8,128)(2,1)}), bf16[128,6144]{1,0:T(8,128)(2,1)}) %reduce-scatter.5.cloned.1.call-update) | async-done | bytes 1572880 | tf_op jit(solution)/shard_map/reduce_scatter | solution.py:838
  457.5 1.3 fusion.58
  458.8 3.4 collective-permute-start.29
  462.2 1.1 collective-permute-start.31
  464.1 7.7 %collective-permute-done.29 = bf16[128,1536]{1,0:T(8,128)(2,1)S(1)} collective-permute-done((bf16[128,1536]{1,0:T(8,128)(2,1)S(1)}, bf16[128,1536]{1,0:T(8,128)(2,1)S(1)}, u32[]{:S(2)}, u32[]{:S(2)}) %collective-permute-start.29) | collective-permute-done | bytes 393248 | tf_op jit(solution)/shard_map/ppermute | solution.py:707
  471.7 24.2 %collective-permute-done.30 = bf16[128,1536]{1,0:T(8,128)(2,1)S(1)} collective-permute-done((bf16[128,1536]{1,0:T(8,128)(2,1)S(1)}, bf16[128,1536]{1,0:T(8,128)(2,1)S(1)}, u32[]{:S(2)}, u32[]{:S(2)}) %collective-permute-start.30) | collective-permute-done | bytes 393248 | tf_op jit(solution)/shard_map/ppermute | solution.py:707
  495.9 1.2 convert_add_fusion.2
  (215 shorter events, 44.9 us)
Async XLA Ops:
  7.2 67.1 %all-gather.3.cloned.1.call-start = ((), (), s32[]{:S(2)}) async-start(), calls=%async_computation.2 | async-start | bytes 4423680 | tf_op jit(solution)/shard_map/all_gather | solution.py:803
  18.0 33.8 %copy-start = (bf16[256,1024]{1,0:T(8,128)(2,1)S(1)}, bf16[256,1024]{1,0:T(8,128)(2,1)}, u32[]{:S(2)}) copy-start(bf16[256,1024]{1,0:T(8,128)(2,1)} %refs_1_.3) | copy-start | bytes 1572868
  18.0 55.4 %copy-start.43 = (f32[384]{0:T(512)S(1)}, f32[384]{0:T(512)}, u32[]{:S(2)}) copy-start(f32[384]{0:T(512)} %param.43) | copy-start | bytes 4612
  18.0 55.4 %copy-start.44 = (f32[256]{0:T(256)S(1)}, f32[256]{0:T(256)}, u32[]{:S(2)}) copy-start(f32[256]{0:T(256)} %param.44) | copy-start | bytes 3076
  19.0 54.4 %copy-start.45 = (f32[6]{0:T(128)S(1)}, f32[6]{0:T(128)}, u32[]{:S(2)}) copy-start(f32[6]{0:T(128)} %param.47) | copy-start | bytes 76
  19.0 54.6 %copy-start.46 = (f32[6]{0:T(128)S(1)}, f32[6]{0:T(128)}, u32[]{:S(2)}) copy-start(f32[6]{0:T(128)} %param.46) | copy-start | bytes 76
  19.0 54.6 %copy-start.47 = (f32[6]{0:T(128)S(1)}, f32[6]{0:T(128)}, u32[]{:S(2)}) copy-start(f32[6]{0:T(128)} %param.45) | copy-start | bytes 76
  19.0 54.6 %copy-start.41 = (f32[4,384]{1,0:T(4,128)S(1)}, f32[4,384]{1,0:T(4,128)}, u32[]{:S(2)}) copy-start(f32[4,384]{1,0:T(4,128)} %param.41) | copy-start | bytes 18436
  19.0 54.6 %copy-start.42 = (f32[4,256]{1,0:T(4,128)S(1)}, f32[4,256]{1,0:T(4,128)}, u32[]{:S(2)}) copy-start(f32[4,256]{1,0:T(4,128)} %param.42) | copy-start | bytes 12292
  19.0 54.6 %copy-start.40 = (s32[1,1024]{1,0:T(1,128)S(1)}, s32[1,1024]{1,0:T(1,128)}, u32[]{:S(2)}) copy-start(s32[1,1024]{1,0:T(1,128)} %param.32) | copy-start | bytes 12292
  19.1 164.4 %all-gather.5.cloned.1.call-start = ((), (), s32[]{:S(2)}) async-start(), calls=%async_computation.3 | async-start | bytes 14155776 | tf_op jit(solution)/shard_map/all_gather | solution.py:809
  19.1 23.4 %collective-permute-start.10 = (bf16[128,1536]{1,0:T(8,128)(2,1)S(1)}, bf16[128,1536]{1,0:T(8,128)(2,1)S(1)}, u32[]{:S(2)}, u32[]{:S(2)}) collective-permute-start(bf16[128,1536]{1,0:T(8,128)(2,1)S(1)} %get-tuple-element.71), channel_id=1, source_target_pairs={{0,2},{1,3},{2,0},{3,1},{4,6},{5,7},{6,4},{7,5},{8,10},{9,11},{10,... | collective-permute-start | bytes 1179656 | tf_op jit(solution)/shard_map/ppermute | solution.py:707
  23.2 19.3 %collective-permute-start.11 = (bf16[128,1536]{1,0:T(8,128)(2,1)S(1)}, bf16[128,1536]{1,0:T(8,128)(2,1)S(1)}, u32[]{:S(2)}, u32[]{:S(2)}) collective-permute-start(bf16[128,1536]{1,0:T(8,128)(2,1)S(1)} %get-tuple-element.71), channel_id=1, source_target_pairs={{0,3},{1,0},{2,1},{3,2},{4,7},{5,4},{6,5},{7,6},{8,11},{9,8},{10,9... | collective-permute-start | bytes 1179656 | tf_op jit(solution)/shard_map/ppermute | solution.py:707
  24.6 25.8 %collective-permute-start.9 = (bf16[128,1536]{1,0:T(8,128)(2,1)S(1)}, bf16[128,1536]{1,0:T(8,128)(2,1)S(1)}, u32[]{:S(2)}, u32[]{:S(2)}) collective-permute-start(bf16[128,1536]{1,0:T(8,128)(2,1)S(1)} %get-tuple-element.71), channel_id=1, source_target_pairs={{0,1},{1,2},{2,3},{3,0},{4,5},{5,6},{6,7},{7,4},{8,9},{9,10},{10,1... | collective-permute-start | bytes 1179656 | tf_op jit(solution)/shard_map/ppermute | solution.py:707
  51.8 339.0 %reduce-scatter.3.cloned.1.call-start = ((), (), s32[]{:S(2)}) async-start(), calls=%async_computation.4 | async-start | bytes 4423680 | tf_op jit(solution)/shard_map/reduce_scatter | solution.py:867
  51.8 31.5 %collective-permute-start = (bf16[256,1024]{1,0:T(8,128)(2,1)S(1)}, bf16[256,1024]{1,0:T(8,128)(2,1)S(1)}, u32[]{:S(2)}, u32[]{:S(2)}) collective-permute-start(bf16[256,1024]{1,0:T(8,128)(2,1)S(1)} %copy-done), channel_id=1, source_target_pairs={{0,1},{1,2},{2,3},{3,0},{4,5},{5,6},{6,7},{7,4},{8,9},{9,10},{10,1... | collective-permute-start | bytes 1572872 | tf_op jit(solution)/shard_map/ppermute | solution.py:707
  71.0 24.9 %collective-permute-start.1 = (bf16[256,1024]{1,0:T(8,128)(2,1)S(1)}, bf16[256,1024]{1,0:T(8,128)(2,1)S(1)}, u32[]{:S(2)}, u32[]{:S(2)}) collective-permute-start(bf16[256,1024]{1,0:T(8,128)(2,1)S(1)} %copy-done), channel_id=1, source_target_pairs={{0,2},{1,3},{2,0},{3,1},{4,6},{5,7},{6,4},{7,5},{8,10},{9,11},{10,... | collective-permute-start | bytes 1572872 | tf_op jit(solution)/shard_map/ppermute | solution.py:707
  71.0 33.1 %collective-permute-start.2 = (bf16[256,1024]{1,0:T(8,128)(2,1)S(1)}, bf16[256,1024]{1,0:T(8,128)(2,1)S(1)}, u32[]{:S(2)}, u32[]{:S(2)}) collective-permute-start(bf16[256,1024]{1,0:T(8,128)(2,1)S(1)} %copy-done), channel_id=1, source_target_pairs={{0,3},{1,0},{2,1},{3,2},{4,7},{5,4},{6,5},{7,6},{8,11},{9,8},{10,9... | collective-permute-start | bytes 1572872 | tf_op jit(solution)/shard_map/ppermute | solution.py:707
  74.3 30.6 %copy-start.33 = (bf16[1024,1920]{1,0:T(8,128)(2,1)S(1)}, bf16[1024,1920]{1,0:T(8,128)(2,1)}, u32[]{:S(2)}) copy-start(bf16[1024,1920]{1,0:T(8,128)(2,1)} %all-gather.3.cloned.1.call-done) | copy-start | bytes 11796484
  104.9 5.2 %copy-start.1 = (bf16[1024,1024]{1,0:T(8,128)(2,1)}, bf16[1024,1024]{1,0:T(8,128)(2,1)S(1)}, u32[]{:S(2)}) copy-start(bf16[1024,1024]{1,0:T(8,128)(2,1)S(1)} %norm_rows.1) | copy-start | bytes 6291460
  110.3 26.0 %copy-start.3 = (s32[1024,128]{1,0:T(8,128)}, s32[1024,128]{1,0:T(8,128)S(1)}, u32[]{:S(2)}) copy-start(s32[1024,128]{1,0:T(8,128)S(1)} %broadcast_in_dim.28.start_ref.refs_1_.refs_2_) | copy-start | bytes 1572868
  110.5 25.8 %copy-start.6 = (f32[1024,128]{1,0:T(8,128)S(1)}, f32[1024,128]{1,0:T(8,128)}, u32[]{:S(2)}) copy-start(f32[1024,128]{1,0:T(8,128)} %constant.125.clone.cos_ref) | copy-start | bytes 1572868
  110.5 25.8 %copy-start.8 = (f32[1024,128]{1,0:T(8,128)S(1)}, f32[1024,128]{1,0:T(8,128)}, u32[]{:S(2)}) copy-start(f32[1024,128]{1,0:T(8,128)} %constant.126.clone.sin_ref) | copy-start | bytes 1572868
  121.5 20.4 %copy-start.29 = (bf16[8,128,384]{2,1,0:T(8,128)(2,1)}, bf16[8,128,384]{2,1,0:T(8,128)(2,1)S(1)}, u32[]{:S(2)}) copy-start(bf16[8,128,384]{2,1,0:T(8,128)(2,1)S(1)} %get-tuple-element.80.refs_10_) | copy-start | bytes 2359300
  121.5 20.5 %copy-start.39 = (f32[384]{0:T(512)S(1)}, f32[384]{0:T(512)}, u32[]{:S(2)}) copy-start(f32[384]{0:T(512)} %param.48) | copy-start | bytes 4612
  121.5 20.4 %collective-permute-start.3 = (f32[1,1024]{1,0:T(1,128)S(1)}, f32[1,1024]{1,0:T(1,128)S(1)}, u32[]{:S(2)}, u32[]{:S(2)}) collective-permute-start(f32[1,1024]{1,0:T(1,128)S(1)} %slice.144), channel_id=1, source_target_pairs={{0,1},{1,2},{2,3},{3,0},{4,5},{5,6},{6,7},{7,4},{8,9},{9,10},{10,1... | collective-permute-start | bytes 12296 | tf_op jit(solution)/shard_map/ppermute | solution.py:707
  132.9 9.0 %collective-permute-start.4 = (f32[1,1024]{1,0:T(1,128)S(1)}, f32[1,1024]{1,0:T(1,128)S(1)}, u32[]{:S(2)}, u32[]{:S(2)}) collective-permute-start(f32[1,1024]{1,0:T(1,128)S(1)} %slice.144), channel_id=1, source_target_pairs={{0,2},{1,3},{2,0},{3,1},{4,6},{5,7},{6,4},{7,5},{8,10},{9,11},{10,... | collective-permute-start | bytes 12296 | tf_op jit(solution)/shard_map/ppermute | solution.py:707
  136.3 5.7 %collective-permute-start.5 = (f32[1,1024]{1,0:T(1,128)S(1)}, f32[1,1024]{1,0:T(1,128)S(1)}, u32[]{:S(2)}, u32[]{:S(2)}) collective-permute-start(f32[1,1024]{1,0:T(1,128)S(1)} %slice.144), channel_id=1, source_target_pairs={{0,3},{1,0},{2,1},{3,2},{4,7},{5,4},{6,5},{7,6},{8,11},{9,8},{10,9... | collective-permute-start | bytes 12296 | tf_op jit(solution)/shard_map/ppermute | solution.py:707
  141.9 4.9 copy-start.21
  141.9 4.9 copy-start.23
  141.9 4.9 copy-start.25
  142.2 38.0 %copy-start.31 = (bf16[1024,384]{1,0:T(8,128)(2,1)}, bf16[1024,384]{1,0:T(8,128)(2,1)S(1)}, u32[]{:S(2)}) copy-start(bf16[1024,384]{1,0:T(8,128)(2,1)S(1)} %multiply_convert_fusion) | copy-start | bytes 2359300
  143.5 17.1 %collective-permute-start.6 = (bf16[256,1024]{1,0:T(8,128)(2,1)}, bf16[256,1024]{1,0:T(8,128)(2,1)}, u32[]{:S(2)}, u32[]{:S(2)}) collective-permute-start(bf16[256,1024]{1,0:T(8,128)(2,1)} %convolution_convert_fusion.3), channel_id=1, source_target_pairs={{0,1},{1,2},{2,3},{3,0},{4,5},{5,6},{6,7},{7,4},{8,9},{9,10},{10,1... | collective-permute-start | bytes 1572872 | tf_op jit(solution)/shard_map/ppermute | solution.py:707
  146.8 33.4 %collective-permute-start.7 = (bf16[256,1024]{1,0:T(8,128)(2,1)}, bf16[256,1024]{1,0:T(8,128)(2,1)}, u32[]{:S(2)}, u32[]{:S(2)}) collective-permute-start(bf16[256,1024]{1,0:T(8,128)(2,1)} %convolution_convert_fusion.2), channel_id=1, source_target_pairs={{0,2},{1,3},{2,0},{3,1},{4,6},{5,7},{6,4},{7,5},{8,10},{9,11},{10,... | collective-permute-start | bytes 1572872 | tf_op jit(solution)/shard_map/ppermute | solution.py:707
  148.2 32.0 %collective-permute-start.8 = (bf16[256,1024]{1,0:T(8,128)(2,1)}, bf16[256,1024]{1,0:T(8,128)(2,1)}, u32[]{:S(2)}, u32[]{:S(2)}) collective-permute-start(bf16[256,1024]{1,0:T(8,128)(2,1)} %convolution_convert_fusion.1), channel_id=1, source_target_pairs={{0,3},{1,0},{2,1},{3,2},{4,7},{5,4},{6,5},{7,6},{8,11},{9,8},{10,9... | collective-permute-start | bytes 1572872 | tf_op jit(solution)/shard_map/ppermute | solution.py:707
  203.1 24.5 %collective-permute-start.12 = (bf16[256,1024]{1,0:T(8,128)(2,1)}, bf16[256,1024]{1,0:T(8,128)(2,1)}, u32[]{:S(2)}, u32[]{:S(2)}) collective-permute-start(bf16[256,1024]{1,0:T(8,128)(2,1)} %convert_element_type.151), channel_id=1, source_target_pairs={{0,3},{1,0},{2,1},{3,2},{4,7},{5,4},{6,5},{7,6},{8,11},{9,8},{10,9... | collective-permute-start | bytes 1572872 | tf_op jit(solution)/shard_map/ppermute | solution.py:707
  214.8 47.3 %collective-permute-start.13 = (bf16[256,1024]{1,0:T(8,128)(2,1)}, bf16[256,1024]{1,0:T(8,128)(2,1)}, u32[]{:S(2)}, u32[]{:S(2)}) collective-permute-start(bf16[256,1024]{1,0:T(8,128)(2,1)} %convert_element_type.151), channel_id=1, source_target_pairs={{0,2},{1,3},{2,0},{3,1},{4,6},{5,7},{6,4},{7,5},{8,10},{9,11},{10,... | collective-permute-start | bytes 1572872 | tf_op jit(solution)/shard_map/ppermute | solution.py:707
  216.3 46.9 %collective-permute-start.14 = (bf16[256,1024]{1,0:T(8,128)(2,1)}, bf16[256,1024]{1,0:T(8,128)(2,1)}, u32[]{:S(2)}, u32[]{:S(2)}) collective-permute-start(bf16[256,1024]{1,0:T(8,128)(2,1)} %convert_element_type.151), channel_id=1, source_target_pairs={{0,1},{1,2},{2,3},{3,0},{4,5},{5,6},{6,7},{7,4},{8,9},{9,10},{10,1... | collective-permute-start | bytes 1572872 | tf_op jit(solution)/shard_map/ppermute | solution.py:707
  271.5 4.8 copy-start.4
  271.5 4.8 copy-start.7
  271.5 4.8 copy-start.9
  271.5 4.8 copy-start.22
  271.5 4.8 copy-start.24
  271.5 4.8 copy-start.26
  272.1 10.9 %collective-permute-start.15 = (f32[1,1024]{1,0:T(1,128)S(1)}, f32[1,1024]{1,0:T(1,128)S(1)}, u32[]{:S(2)}, u32[]{:S(2)}) collective-permute-start(f32[1,1024]{1,0:T(1,128)S(1)} %bitcast.36), channel_id=1, source_target_pairs={{0,1},{1,2},{2,3},{3,0},{4,5},{5,6},{6,7},{7,4},{8,9},{9,10},{10,1... | collective-permute-start | bytes 12296 | tf_op jit(solution)/shard_map/ppermute | solution.py:707
  272.2 10.9 %collective-permute-start.16 = (f32[1,1024]{1,0:T(1,128)S(1)}, f32[1,1024]{1,0:T(1,128)S(1)}, u32[]{:S(2)}, u32[]{:S(2)}) collective-permute-start(f32[1,1024]{1,0:T(1,128)S(1)} %bitcast.37), channel_id=1, source_target_pairs={{0,2},{1,3},{2,0},{3,1},{4,6},{5,7},{6,4},{7,5},{8,10},{9,11},{10,... | collective-permute-start | bytes 12296 | tf_op jit(solution)/shard_map/ppermute | solution.py:707
  272.3 10.8 %collective-permute-start.17 = (f32[1,1024]{1,0:T(1,128)S(1)}, f32[1,1024]{1,0:T(1,128)S(1)}, u32[]{:S(2)}, u32[]{:S(2)}) collective-permute-start(f32[1,1024]{1,0:T(1,128)S(1)} %bitcast.38), channel_id=1, source_target_pairs={{0,3},{1,0},{2,1},{3,2},{4,7},{5,4},{6,5},{7,6},{8,11},{9,8},{10,9... | collective-permute-start | bytes 12296 | tf_op jit(solution)/shard_map/ppermute | solution.py:707
  312.0 145.4 %reduce-scatter.5.cloned.1.call-start = ((), (), s32[]{:S(2)}) async-start(), calls=%async_computation.5 | async-start | bytes 14155776 | tf_op jit(solution)/shard_map/reduce_scatter | solution.py:838
  312.6 6.4 %copy-start.34 = (bf16[1024,1920]{1,0:T(8,128)(2,1)S(1)}, bf16[1024,1920]{1,0:T(8,128)(2,1)}, u32[]{:S(2)}) copy-start(bf16[1024,1920]{1,0:T(8,128)(2,1)} %all-gather.3.cloned.1.call-done) | copy-start | bytes 11796484
  317.0 27.3 %collective-permute-start.19 = (bf16[256,1024]{1,0:T(8,128)(2,1)}, bf16[256,1024]{1,0:T(8,128)(2,1)S(1)}, u32[]{:S(2)}, u32[]{:S(2)}) collective-permute-start(bf16[256,1024]{1,0:T(8,128)(2,1)} %get-tuple-element.186), channel_id=1, source_target_pairs={{0,2},{1,3},{2,0},{3,1},{4,6},{5,7},{6,4},{7,5},{8,10},{9,11},{10,... | collective-permute-start | bytes 1572872 | tf_op jit(solution)/shard_map/ppermute | solution.py:707
  322.5 34.3 %collective-permute-start.20 = (bf16[256,1024]{1,0:T(8,128)(2,1)}, bf16[256,1024]{1,0:T(8,128)(2,1)S(1)}, u32[]{:S(2)}, u32[]{:S(2)}) collective-permute-start(bf16[256,1024]{1,0:T(8,128)(2,1)} %get-tuple-element.184), channel_id=1, source_target_pairs={{0,3},{1,0},{2,1},{3,2},{4,7},{5,4},{6,5},{7,6},{8,11},{9,8},{10,9... | collective-permute-start | bytes 1572872 | tf_op jit(solution)/shard_map/ppermute | solution.py:707
  326.7 30.1 %collective-permute-start.18 = (bf16[256,1024]{1,0:T(8,128)(2,1)}, bf16[256,1024]{1,0:T(8,128)(2,1)S(1)}, u32[]{:S(2)}, u32[]{:S(2)}) collective-permute-start(bf16[256,1024]{1,0:T(8,128)(2,1)} %get-tuple-element.188), channel_id=1, source_target_pairs={{0,1},{1,2},{2,3},{3,0},{4,5},{5,6},{6,7},{7,4},{8,9},{9,10},{10,1... | collective-permute-start | bytes 1572872 | tf_op jit(solution)/shard_map/ppermute | solution.py:707
  363.4 1.3 collective-permute-start.21
  364.8 4.3 collective-permute-start.22
  369.1 4.3 collective-permute-start.23
  373.5 10.4 %collective-permute-start.24 = (f32[16,1024]{1,0:T(8,128)S(1)}, f32[16,1024]{1,0:T(8,128)S(1)}, u32[]{:S(2)}, u32[]{:S(2)}) collective-permute-start(f32[16,1024]{1,0:T(8,128)S(1)} %add.242), channel_id=1, source_target_pairs={{0,1},{1,0},{2,3},{3,2},{4,5},{5,4},{6,7},{7,6},{8,9},{9,8},{10,11... | collective-permute-start | bytes 196616 | tf_op jit(solution)/shard_map/ppermute | solution.py:737
  383.8 5.2 %collective-permute-start.25 = (f32[16,1024]{1,0:T(8,128)S(1)}, f32[16,1024]{1,0:T(8,128)S(1)}, u32[]{:S(2)}, u32[]{:S(2)}) collective-permute-start(f32[16,1024]{1,0:T(8,128)S(1)} %add.243), channel_id=1, source_target_pairs={{0,2},{1,3},{2,0},{3,1},{4,6},{5,7},{6,4},{7,5},{8,10},{9,11},{10,... | collective-permute-start | bytes 196616 | tf_op jit(solution)/shard_map/ppermute | solution.py:737
  390.8 9.7 %copy-start.35 = (bf16[128,1920]{1,0:T(8,128)(2,1)S(1)}, bf16[128,1920]{1,0:T(8,128)(2,1)}, u32[]{:S(2)}) copy-start(bf16[128,1920]{1,0:T(8,128)(2,1)} %reduce-scatter.3.cloned.1.call-done) | copy-start | bytes 1474564
  393.1 69.1 %collective-permute-start.26 = (bf16[128,512]{1,0:T(8,128)(2,1)S(1)}, bf16[128,512]{1,0:T(8,128)(2,1)S(1)}, u32[]{:S(2)}, u32[]{:S(2)}) collective-permute-start(bf16[128,512]{1,0:T(8,128)(2,1)S(1)} %pad_maximum_fusion.4), channel_id=1, source_target_pairs={{0,1},{1,2},{2,3},{3,0},{4,5},{5,6},{6,7},{7,4},{8,9},{9,10},{10,1... | collective-permute-start | bytes 393224 | tf_op jit(solution)/shard_map/ppermute | solution.py:707
  395.3 67.9 %collective-permute-start.27 = (bf16[128,512]{1,0:T(8,128)(2,1)S(1)}, bf16[128,512]{1,0:T(8,128)(2,1)S(1)}, u32[]{:S(2)}, u32[]{:S(2)}) collective-permute-start(bf16[128,512]{1,0:T(8,128)(2,1)S(1)} %pad_maximum_fusion.4), channel_id=1, source_target_pairs={{0,2},{1,3},{2,0},{3,1},{4,6},{5,7},{6,4},{7,5},{8,10},{9,11},{10,... | collective-permute-start | bytes 393224 | tf_op jit(solution)/shard_map/ppermute | solution.py:707
  396.5 66.8 %collective-permute-start.28 = (bf16[128,512]{1,0:T(8,128)(2,1)S(1)}, bf16[128,512]{1,0:T(8,128)(2,1)S(1)}, u32[]{:S(2)}, u32[]{:S(2)}) collective-permute-start(bf16[128,512]{1,0:T(8,128)(2,1)S(1)} %pad_maximum_fusion.4), channel_id=1, source_target_pairs={{0,3},{1,0},{2,1},{3,2},{4,7},{5,4},{6,5},{7,6},{8,11},{9,8},{10,9... | collective-permute-start | bytes 393224 | tf_op jit(solution)/shard_map/ppermute | solution.py:707
  458.8 12.9 %collective-permute-start.29 = (bf16[128,1536]{1,0:T(8,128)(2,1)S(1)}, bf16[128,1536]{1,0:T(8,128)(2,1)S(1)}, u32[]{:S(2)}, u32[]{:S(2)}) collective-permute-start(bf16[128,1536]{1,0:T(8,128)(2,1)S(1)} %get-tuple-element.168), channel_id=1, source_target_pairs={{0,3},{1,0},{2,1},{3,2},{4,7},{5,4},{6,5},{7,6},{8,11},{9,8},{10,9... | collective-permute-start | bytes 1179656 | tf_op jit(solution)/shard_map/ppermute | solution.py:707
  462.2 33.7 %collective-permute-start.30 = (bf16[128,1536]{1,0:T(8,128)(2,1)S(1)}, bf16[128,1536]{1,0:T(8,128)(2,1)S(1)}, u32[]{:S(2)}, u32[]{:S(2)}) collective-permute-start(bf16[128,1536]{1,0:T(8,128)(2,1)S(1)} %get-tuple-element.170), channel_id=1, source_target_pairs={{0,2},{1,3},{2,0},{3,1},{4,6},{5,7},{6,4},{7,5},{8,10},{9,11},{10,... | collective-permute-start | bytes 1179656 | tf_op jit(solution)/shard_map/ppermute | solution.py:707
  462.2 33.7 %collective-permute-start.31 = (bf16[128,1536]{1,0:T(8,128)(2,1)S(1)}, bf16[128,1536]{1,0:T(8,128)(2,1)S(1)}, u32[]{:S(2)}, u32[]{:S(2)}) collective-permute-start(bf16[128,1536]{1,0:T(8,128)(2,1)S(1)} %get-tuple-element.169), channel_id=1, source_target_pairs={{0,1},{1,2},{2,3},{3,0},{4,5},{5,6},{6,7},{7,4},{8,9},{9,10},{10,1... | collective-permute-start | bytes 1179656 | tf_op jit(solution)/shard_map/ppermute | solution.py:707
  (20 other events, 27.4 us)
Sparse Core Ops, SparseCore 0:
  19.2 38.3 all-gather.2
  59.4 81.3 all-gather.4
  312.2 49.0 reduce-scatter.2
  365.1 92.3 reduce-scatter.4
